TPU v7x, 32 devices: a whole 2x2x4 slice. The times are simulated.
32 devices in a mesh: dp: 8 (over z, x), tensor: 4 (over y, core).
Axes of the slice: x: 2, y: 2, z: 4, core: 2. Of those that a mesh axis runs over, the one named last changes fastest.
Arguments:
- tokens: bfloat16 [8192, 768], P(('dp', 'tensor')), may hold values from -6 to 6
- final_output_gradient: bfloat16 [8192, 768], P(('dp', 'tensor')), may hold values from -6 to 6
- lengths: int32 [8, 32], P('dp'), may hold values from 0 to 512, as said below
- query_key_value_weight: bfloat16 [2, 3, 768, 768], P(None, None, 'dp', 'tensor'), may hold values from -0.21875 to 0.21875
- output_projection_weight: bfloat16 [2, 768, 768], P(None, 'dp', 'tensor'), may hold values from -0.625 to 0.625
- biases: float32 [2, 6, 768], replicated, may hold values from -2.5 to 2.5
- frozen_norm_gains: float32 [2, 2, 768], replicated, may hold values from 0.5 to 1.5
- feedforward_in_weight: bfloat16 [2, 768, 3072], P(None, None, 'tensor'), may hold values from -0.21875 to 0.21875
- feedforward_bias: bfloat16 [2, 3072], P(None, 'tensor'), may hold values from -2.5 to 2.5
- feedforward_out_weight: bfloat16 [2, 3072, 768], P(None, 'tensor'), may hold values from -0.109375 to 0.109375
- adapter_down_weights: bfloat16 [2, 2, 768, 8], replicated, may hold values from -0.21875 to 0.21875
- adapter_up_weights: bfloat16 [2, 2, 8, 768], replicated, may hold values from -2 to 2
Outputs:
- activations: bfloat16 [8192, 768], P(('dp', 'tensor'))
- input_grad: bfloat16 [8192, 768], P(('dp', 'tensor'))
- lora_a_grad: float32 [2, 2, 768, 8], replicated
- lora_b_grad: float32 [2, 2, 8, 768], replicated
Inputs may be any that keep to these rules, and one draw needn't show every extreme that they name: Row g lists the lengths of the sequences packed in order into the 1024 rows of group g; the nonzero entries form a prefix whose sum is at most 1024, the rows past it being padding; a length of 512 occurs in every draw.
All inputs are finite; a program needn't handle non-finite values.
Results may differ from a plain program's by a relative error of at most 0.035.
Values may be sent and summed in bfloat16 or wider, within the bound.
No kernel may reach another device: no remote copies, remote signals or barrier semaphores. Data moves between devices by JAX's collectives and lax.ppermute only.
A program may use at most 128 MiB of HBM per device.

v0:
```python
import jax
import jax.numpy as jnp
from jax import lax
from jax.sharding import PartitionSpec as P

MODEL_WIDTH = 768
HEAD_DIM = 64
ADAPTER_RANK = 8
ENCODER_LAYERS = 2


epsilon = 1e-05
adapter_scale = 2.0
masked_score = -1000000000.0
exact_prec = lax.Precision.HIGHEST


def normalize(row_data, gain_row, shift_row):
    row_mean = jnp.mean(row_data, axis=-1, keepdims=True)
    centered = row_data - row_mean
    variance = jnp.mean(centered * centered, axis=-1, keepdims=True)
    return centered * lax.rsqrt(variance + epsilon) * gain_row + shift_row


def exact_gelu(values_in):
    return jax.nn.gelu(values_in, approximate=False)


def segment_of(lengths_row, group_len):
    seg_ends = jnp.cumsum(lengths_row)
    position = jnp.arange(group_len, dtype=jnp.int32)
    return jnp.sum((seg_ends[None, :] <= position[:, None]).astype(jnp.int32), axis=1)


def block_scores(query_block, key_rows, segment_block, segment):
    scores = jnp.einsum(
        "qhd,khd->hqk", query_block, key_rows, preferred_element_type=jnp.float32
    ) * HEAD_DIM ** (-0.5)
    same_seg = segment_block[:, None] == segment[None, :]
    return jnp.where(same_seg[None], scores, masked_score)


def attend(rows_of_queries, key_rows, rows_of_values, segment, block_len):
    group_len = rows_of_queries.shape[0]

    def one_block(block_index):
        row_start = block_index * block_len
        query_block = lax.dynamic_slice_in_dim(rows_of_queries, row_start, block_len, 0)
        segment_block = lax.dynamic_slice_in_dim(segment, row_start, block_len, 0)
        scores = block_scores(query_block, key_rows, segment_block, segment)
        top_score = jnp.max(scores, axis=-1, keepdims=True)
        weights = jnp.exp(scores - top_score)
        row_total = jnp.sum(weights, axis=-1, keepdims=True)
        prob_low = (weights / row_total).astype(jnp.bfloat16)
        context = jnp.einsum(
            "hqk,khd->qhd", prob_low, rows_of_values, preferred_element_type=jnp.float32
        )
        return (context.astype(jnp.bfloat16), (top_score + jnp.log(row_total))[..., 0])

    context, logsum = lax.map(one_block, jnp.arange(group_len // block_len, dtype=jnp.int32))
    return (context.reshape(group_len, -1), logsum)


def attend_back(
    rows_of_queries, key_rows, rows_of_values, segment, logsum, grad_context, block_len
):
    group_len = rows_of_queries.shape[0]
    scale = HEAD_DIM ** (-0.5)

    def one_block(carry, block_index):
        grad_keys, grad_values = carry
        row_start = block_index * block_len
        query_block = lax.dynamic_slice_in_dim(rows_of_queries, row_start, block_len, 0)
        segment_block = lax.dynamic_slice_in_dim(segment, row_start, block_len, 0)
        grad_block = lax.dynamic_slice_in_dim(grad_context, row_start, block_len, 0)
        scores = block_scores(query_block, key_rows, segment_block, segment)
        probs_full = jnp.exp(scores - logsum[block_index][..., None])
        grad_probs = jnp.einsum(
            "qhd,khd->hqk", grad_block, rows_of_values, preferred_element_type=jnp.float32
        )
        delta_row = jnp.sum(probs_full * grad_probs, axis=-1, keepdims=True)
        grad_scores = (probs_full * (grad_probs - delta_row)).astype(jnp.bfloat16)
        grad_query = (
            jnp.einsum("hqk,khd->qhd", grad_scores, key_rows, preferred_element_type=jnp.float32)
            * scale
        )
        grad_keys = (
            grad_keys
            + jnp.einsum(
                "hqk,qhd->khd", grad_scores, query_block, preferred_element_type=jnp.float32
            )
            * scale
        )
        grad_values = grad_values + jnp.einsum(
            "hqk,qhd->khd",
            probs_full.astype(jnp.bfloat16),
            grad_block,
            preferred_element_type=jnp.float32,
        )
        return ((grad_keys, grad_values), grad_query.astype(jnp.bfloat16))

    zero_init = jnp.zeros(key_rows.shape, jnp.float32)
    (grad_keys, grad_values), grad_query = lax.scan(
        one_block, (zero_init, zero_init), jnp.arange(group_len // block_len, dtype=jnp.int32)
    )
    return (
        grad_query.reshape(group_len, -1),
        grad_keys.reshape(group_len, -1).astype(jnp.bfloat16),
        grad_values.reshape(group_len, -1).astype(jnp.bfloat16),
    )


def body(
    tokens,
    final_output_gradient,
    lengths,
    query_key_value_weight,
    output_projection_weight,
    biases,
    frozen_norm_gains,
    feedforward_in_weight,
    feedforward_bias,
    feedforward_out_weight,
    adapter_down_weights,
    adapter_up_weights,
):
    rows_dev = tokens.shape[0]
    tensor_size = lax.axis_size("tensor")
    group_len = rows_dev * tensor_size
    block_len = min(512, group_len)
    segment = segment_of(lengths[0], group_len)
    col_width = query_key_value_weight.shape[-1]
    column = lax.axis_index("tensor") * col_width
    heads_here = col_width // HEAD_DIM

    def split_heads(block_data):
        return block_data.reshape(group_len, heads_here, HEAD_DIM)

    def local_columns(vector):
        return lax.dynamic_slice_in_dim(vector, column, col_width, vector.ndim - 1)

    def frozen_weights(current_layer_index):
        gathered = (
            lax.all_gather(query_key_value_weight[current_layer_index], "dp", axis=1, tiled=True),
            lax.all_gather(output_projection_weight[current_layer_index], "dp", axis=0, tiled=True),
        )
        return gathered

    def projections_of(
        segment_group_rows,
        head_projections,
        current_layer_index,
        query_up_weight,
        value_up_weight,
        bias_q,
        bias_v,
    ):
        query_down_weight = jnp.dot(
            segment_group_rows,
            adapter_down_weights[current_layer_index, 0],
            preferred_element_type=jnp.float32,
        ).astype(jnp.bfloat16)
        value_down_weight = jnp.dot(
            segment_group_rows,
            adapter_down_weights[current_layer_index, 1],
            preferred_element_type=jnp.float32,
        ).astype(jnp.bfloat16)
        rows_of_queries = (
            jnp.dot(segment_group_rows, head_projections[0], preferred_element_type=jnp.float32)
            + bias_q
            + adapter_scale
            * jnp.dot(query_down_weight, query_up_weight, preferred_element_type=jnp.float32)
        ).astype(jnp.bfloat16)
        key_rows = jnp.dot(
            segment_group_rows, head_projections[1], preferred_element_type=jnp.float32
        ).astype(jnp.bfloat16)
        rows_of_values = (
            jnp.dot(segment_group_rows, head_projections[2], preferred_element_type=jnp.float32)
            + bias_v
            + adapter_scale
            * jnp.dot(value_down_weight, value_up_weight, preferred_element_type=jnp.float32)
        ).astype(jnp.bfloat16)
        return (query_down_weight, value_down_weight, rows_of_queries, key_rows, rows_of_values)

    def layer_forward(layer_rows, current_layer_index, weights):
        head_projections, out_proj = weights
        segment_group_rows = lax.all_gather(layer_rows, "tensor", axis=0, tiled=True)
        query_up_weight = local_columns(adapter_up_weights[current_layer_index, 0])
        value_up_weight = local_columns(adapter_up_weights[current_layer_index, 1])
        query_down_weight, value_down_weight, rows_of_queries, key_rows, rows_of_values = (
            projections_of(
                segment_group_rows,
                head_projections,
                current_layer_index,
                query_up_weight,
                value_up_weight,
                local_columns(biases[current_layer_index, 0]),
                local_columns(biases[current_layer_index, 1]),
            )
        )
        context, logsum = attend(
            split_heads(rows_of_queries),
            split_heads(key_rows),
            split_heads(rows_of_values),
            segment,
            block_len,
        )
        piece_rows = context
        attn_out = lax.psum_scatter(
            jnp.einsum("rc,dc->rd", piece_rows, out_proj, preferred_element_type=jnp.float32),
            "tensor",
            scatter_dimension=0,
            tiled=True,
        )
        first_sum = layer_rows.astype(jnp.float32) + attn_out + biases[current_layer_index, 2]
        normed = normalize(
            first_sum, frozen_norm_gains[current_layer_index, 0], biases[current_layer_index, 3]
        )
        normed_low = normed.astype(jnp.bfloat16)
        in_full = feedforward_in_weight[current_layer_index]
        out_full = feedforward_out_weight[current_layer_index]
        bias_here = feedforward_bias[current_layer_index].astype(jnp.float32)
        pre_act = (
            jnp.dot(
                lax.all_gather(normed_low, "tensor", axis=0, tiled=True),
                in_full,
                preferred_element_type=jnp.float32,
            )
            + bias_here
        )
        hidden = exact_gelu(pre_act).astype(jnp.bfloat16)
        piece_rows = hidden
        branch = lax.psum_scatter(
            jnp.dot(piece_rows, out_full, preferred_element_type=jnp.float32),
            "tensor",
            scatter_dimension=0,
            tiled=True,
        )
        second_sum = normed + branch + biases[current_layer_index, 4]
        output = normalize(
            second_sum, frozen_norm_gains[current_layer_index, 1], biases[current_layer_index, 5]
        )
        kept_state = (
            segment_group_rows,
            query_down_weight,
            value_down_weight,
            query_up_weight,
            value_up_weight,
            rows_of_queries,
            key_rows,
            rows_of_values,
            logsum,
            first_sum,
            pre_act,
            second_sum,
            in_full,
            out_full,
        )
        return (output, kept_state)

    def layer_backward(grad_out, current_layer_index, weights, kept_state):
        head_projections, out_proj = weights
        (
            segment_group_rows,
            query_down_weight,
            value_down_weight,
            query_up_weight,
            value_up_weight,
            rows_of_queries,
            key_rows,
            rows_of_values,
            logsum,
            first_sum,
            pre_act,
            second_sum,
            in_full,
            out_full,
        ) = kept_state

        def norm_second(row_data):
            return normalize(
                row_data, frozen_norm_gains[current_layer_index, 1], biases[current_layer_index, 5]
            )

        def norm_first(row_data):
            return normalize(
                row_data, frozen_norm_gains[current_layer_index, 0], biases[current_layer_index, 3]
            )

        grad_second = jax.vjp(norm_second, second_sum)[1](grad_out)[0]
        grad_low = grad_second.astype(jnp.bfloat16)
        grad_hidden = jnp.einsum(
            "rd,fd->rf",
            lax.all_gather(grad_low, "tensor", axis=0, tiled=True),
            out_full,
            preferred_element_type=jnp.float32,
        )
        grad_pre = jax.vjp(exact_gelu, pre_act)[1](grad_hidden)[0].astype(jnp.bfloat16)
        grad_normed = grad_second + lax.psum_scatter(
            jnp.einsum("rf,df->rd", grad_pre, in_full, preferred_element_type=jnp.float32),
            "tensor",
            scatter_dimension=0,
            tiled=True,
        )
        grad_first = jax.vjp(norm_first, first_sum)[1](grad_normed)[0]
        grad_attn = lax.all_gather(grad_first.astype(jnp.bfloat16), "tensor", axis=0, tiled=True)
        grad_context = jnp.einsum(
            "rd,dc->rc", grad_attn, out_proj, preferred_element_type=jnp.float32
        ).astype(jnp.bfloat16)
        grad_query, grad_keys, grad_values = attend_back(
            split_heads(rows_of_queries),
            split_heads(key_rows),
            split_heads(rows_of_values),
            segment,
            logsum,
            split_heads(grad_context),
            block_len,
        )
        query_down_gradient = adapter_scale * jnp.einsum(
            "rc,kc->rk", grad_query, query_up_weight, preferred_element_type=jnp.float32
        )
        value_down_gradient = adapter_scale * jnp.einsum(
            "rc,kc->rk", grad_values, value_up_weight, preferred_element_type=jnp.float32
        )
        grad_a = jnp.stack(
            [
                jnp.einsum(
                    "rd,rk->dk",
                    segment_group_rows,
                    query_down_gradient,
                    precision=exact_prec,
                    preferred_element_type=jnp.float32,
                ),
                jnp.einsum(
                    "rd,rk->dk",
                    segment_group_rows,
                    value_down_gradient,
                    precision=exact_prec,
                    preferred_element_type=jnp.float32,
                ),
            ]
        )
        local_up_gradient = adapter_scale * jnp.stack(
            [
                jnp.einsum(
                    "rk,rc->kc", query_down_weight, grad_query, preferred_element_type=jnp.float32
                ),
                jnp.einsum(
                    "rk,rc->kc", value_down_weight, grad_values, preferred_element_type=jnp.float32
                ),
            ]
        )
        query_adapter = adapter_down_weights[current_layer_index, 0].astype(jnp.float32)
        value_adapter = adapter_down_weights[current_layer_index, 1].astype(jnp.float32)
        grad_b = lax.dynamic_update_slice_in_dim(
            jnp.zeros((2, ADAPTER_RANK, MODEL_WIDTH), jnp.float32), local_up_gradient, column, 2
        )
        term_sum = jnp.einsum(
            "rc,dc->rd", grad_query, head_projections[0], preferred_element_type=jnp.float32
        )
        term_sum = term_sum + jnp.einsum(
            "rc,dc->rd", grad_keys, head_projections[1], preferred_element_type=jnp.float32
        )
        term_sum = term_sum + jnp.einsum(
            "rc,dc->rd", grad_values, head_projections[2], preferred_element_type=jnp.float32
        )
        term_sum = term_sum + jnp.einsum(
            "rk,dk->rd", query_down_gradient, query_adapter, precision=exact_prec
        )
        term_sum = term_sum + jnp.einsum(
            "rk,dk->rd", value_down_gradient, value_adapter, precision=exact_prec
        )
        grad_rows = grad_first + lax.psum_scatter(
            term_sum, "tensor", scatter_dimension=0, tiled=True
        )
        return (grad_rows, grad_a, grad_b)

    saved_inputs = []
    layer_rows = tokens
    for current_layer_index in range(ENCODER_LAYERS):
        weights = frozen_weights(current_layer_index)
        saved_inputs.append(layer_rows)
        output, kept_state = layer_forward(layer_rows, current_layer_index, weights)
        layer_rows = output.astype(jnp.bfloat16)
    grad_rows = final_output_gradient.astype(jnp.float32)
    list_a = [None] * ENCODER_LAYERS
    list_b = [None] * ENCODER_LAYERS
    for current_layer_index in reversed(range(ENCODER_LAYERS)):
        weights = frozen_weights(current_layer_index)
        output, kept_state = layer_forward(
            saved_inputs[current_layer_index], current_layer_index, weights
        )
        grad_rows, grad_a, grad_b = layer_backward(
            grad_rows, current_layer_index, weights, kept_state
        )
        grad_a, grad_b = lax.psum((grad_a, grad_b), ("dp", "tensor"))
        list_a[current_layer_index] = grad_a
        list_b[current_layer_index] = grad_b
    grad_a_all = jnp.stack(list_a)
    grad_b_all = jnp.stack(list_b)
    return (layer_rows, grad_rows.astype(jnp.bfloat16), grad_a_all, grad_b_all)


def solution(mesh):
    return jax.shard_map(
        body,
        mesh=mesh,
        in_specs=(
            P(("dp", "tensor"), None),
            P(("dp", "tensor"), None),
            P("dp", None),
            P(None, None, "dp", "tensor"),
            P(None, "dp", "tensor"),
            P(),
            P(),
            P(None, None, "tensor"),
            P(None, "tensor"),
            P(None, "tensor", None),
            P(),
            P(),
        ),
        out_specs=(P(("dp", "tensor"), None), P(("dp", "tensor"), None), P(), P()),
        check_vma=False,
    )
```

profile of v0, /device:TPU:0, one launch (start us, length us, event | category | flops | bytes accessed | tf_op | source)
XLA Modules:
  0.0 1183.2 jit_solution(5140018852595894978)
XLA Ops:
  12.6 32.9 %all-gather.1 = bf16[1,768,192]{2,1,0:T(8,128)(2,1)S(1)} all-gather(bf16[1,96,192]{2,1,0:T(8,128)(2,1)S(1)} %get-tuple-element.529), channel_id=3, replica_groups=mesh['dp'=8,'tensor'=4] {'dp'}, dimensions={1}, use_global_device_ids=true | all-gather | bytes 331776 | tf_op jit(solution)/shard_map/all_gather | solution.py:145
  48.6 34.0 %all-gather = bf16[1,3,768,192]{3,2,1,0:T(8,128)(2,1)S(1)} all-gather(bf16[1,3,96,192]{3,2,1,0:T(8,128)(2,1)S(1)} %get-tuple-element.527), channel_id=2, replica_groups=mesh['dp'=8,'tensor'=4] {'dp'}, dimensions={2}, use_global_device_ids=true | all-gather | bytes 995328 | tf_op jit(solution)/shard_map/all_gather | solution.py:144
  89.9 21.0 %while.74 = (s32[]{:T(128)}, bf16[2,512,3,64]{1,3,2,0:T(8,128)(2,1)S(1)}, s32[2]{0:T(128)S(1)}, s32[1024]{0:T(1024)S(1)}, bf16[1024,3,64]{0,2,1:T(8,128)(2,1)S(1...) while((s32[]{:T(128)}, ...), condition=%wide.region_5.6_spmd, body=%wide.region_2.5_spmd.sunk | while | flops 412713984 | bytes 14835891 | solution.py:60
  132.2 20.2 %reduce-scatter.13.cloned.1.call-done = f32[256,768]{1,0:T(8,128)} async-done(((f32[1024,768]{1,0:T(8,128)}), f32[256,768]{1,0:T(8,128)}) %reduce-scatter.13.cloned.1.call-update) | async-done | bytes 786448 | tf_op jit(solution)/shard_map/reduce_scatter | solution.py:209
  153.8 39.3 %reduce-scatter.29.cloned.1.call-done = f32[256,768]{1,0:T(8,128)} async-done(((f32[1024,768]{1,0:T(8,128)}), f32[256,768]{1,0:T(8,128)}) %reduce-scatter.29.cloned.1.call-update) | async-done | bytes 786448 | tf_op jit(solution)/shard_map/reduce_scatter | solution.py:209
  250.6 27.7 %reduce-scatter.31.cloned.1.call-done = f32[256,768]{1,0:T(8,128)} async-done(((f32[1024,768]{1,0:T(8,128)}), f32[256,768]{1,0:T(8,128)}) %reduce-scatter.31.cloned.1.call-update) | async-done | bytes 786448 | tf_op jit(solution)/shard_map/reduce_scatter | solution.py:233
  278.3 40.7 %reduce-scatter.15.cloned.1.call-done = f32[256,768]{1,0:T(8,128)} async-done(((f32[1024,768]{1,0:T(8,128)}), f32[256,768]{1,0:T(8,128)}) %reduce-scatter.15.cloned.1.call-update) | async-done | bytes 786448 | tf_op jit(solution)/shard_map/reduce_scatter | solution.py:233
  325.0 31.2 %all-gather.3 = bf16[1,768,192]{2,1,0:T(8,128)(2,1)S(1)} all-gather(bf16[1,96,192]{2,1,0:T(8,128)(2,1)S(1)} %copy-done.62), channel_id=5, replica_groups=mesh['dp'=8,'tensor'=4] {'dp'}, dimensions={1}, use_global_device_ids=true | all-gather | bytes 331776 | tf_op jit(solution)/shard_map/all_gather | solution.py:145
  356.2 34.6 %all-gather.2 = bf16[1,3,768,192]{3,2,1,0:T(8,128)(2,1)S(1)} all-gather(bf16[1,3,96,192]{3,2,1,0:T(8,128)(2,1)S(1)} %copy-done.53), channel_id=4, replica_groups=mesh['dp'=8,'tensor'=4] {'dp'}, dimensions={2}, use_global_device_ids=true | all-gather | bytes 995328 | tf_op jit(solution)/shard_map/all_gather | solution.py:144
  401.2 21.2 %while.75 = (s32[]{:T(128)}, bf16[2,512,3,64]{1,3,2,0:T(8,128)(2,1)S(1)}, s32[2]{0:T(128)S(1)}, s32[1024]{0:T(1024)S(1)}, bf16[1024,3,64]{0,2,1:T(8,128)(2,1)S(1...) while((s32[]{:T(128)}, ...), condition=%wide.region_15.16_spmd, body=%wide.region_12.15_spmd.sunk | while | flops 412713984 | bytes 14835891 | solution.py:60
  442.9 20.2 %reduce-scatter.17.cloned.1.call-done = f32[256,768]{1,0:T(8,128)} async-done(((f32[1024,768]{1,0:T(8,128)}), f32[256,768]{1,0:T(8,128)}) %reduce-scatter.17.cloned.1.call-update) | async-done | bytes 786448 | tf_op jit(solution)/shard_map/reduce_scatter | solution.py:209
  465.2 38.4 %reduce-scatter.21.cloned.1.call-done = f32[256,768]{1,0:T(8,128)} async-done(((f32[1024,768]{1,0:T(8,128)}), f32[256,768]{1,0:T(8,128)}) %reduce-scatter.21.cloned.1.call-update) | async-done | bytes 786448 | tf_op jit(solution)/shard_map/reduce_scatter | solution.py:209
  562.6 27.9 %reduce-scatter.23.cloned.1.call-done = f32[256,768]{1,0:T(8,128)} async-done(((f32[1024,768]{1,0:T(8,128)}), f32[256,768]{1,0:T(8,128)}) %reduce-scatter.23.cloned.1.call-update) | async-done | bytes 786448 | tf_op jit(solution)/shard_map/reduce_scatter | solution.py:233
  590.5 40.5 %reduce-scatter.19.cloned.1.call-done = f32[256,768]{1,0:T(8,128)} async-done(((f32[1024,768]{1,0:T(8,128)}), f32[256,768]{1,0:T(8,128)}) %reduce-scatter.19.cloned.1.call-update) | async-done | bytes 786448 | tf_op jit(solution)/shard_map/reduce_scatter | solution.py:233
  636.0 19.8 %all-gather.25.cloned.1.call-done = bf16[1024,768]{1,0:T(8,128)(2,1)} async-done(((bf16[256,768]{1,0:T(8,128)(2,1)}), bf16[1024,768]{1,0:T(8,128)(2,1)}) %all-gather.25.cloned.1.call-update) | async-done | bytes 1572880 | tf_op jit(solution)/shard_map/all_gather | solution.py:294
  664.5 38.0 %reduce-scatter.25.cloned.1.call-done = f32[256,768]{1,0:T(8,128)} async-done(((f32[1024,768]{1,0:T(8,128)}), f32[256,768]{1,0:T(8,128)}) %reduce-scatter.25.cloned.1.call-update) | async-done | bytes 786448 | tf_op jit(solution)/shard_map/reduce_scatter | solution.py:299
  706.7 19.7 %all-gather.27.cloned.1.call-done = bf16[1024,768]{1,0:T(8,128)(2,1)} async-done(((bf16[256,768]{1,0:T(8,128)(2,1)}), bf16[1024,768]{1,0:T(8,128)(2,1)}) %all-gather.27.cloned.1.call-update) | async-done | bytes 1572880 | tf_op jit(solution)/shard_map/all_gather | solution.py:306
  729.9 54.0 %while.78 = (s32[]{:T(128)}, f32[1024,3,64]{0,2,1:T(8,128)}, f32[1024,3,64]{0,2,1:T(8,128)}, bf16[2,512,3,64]{1,3,2,0:T(8,128)(2,1)}, s32[2]{0:T(128)}, /*index=...) while((s32[]{:T(128)}, f32[1024,3,64]{0,2,1:T(8,128)}, ...), condition=%wide.region_39.40_spmd.clone, body=%wide.region_37.39_spmd.clone.sunk | while | flops 1031928320 | bytes 90298992 | solution.py:103
  797.5 37.5 %reduce-scatter.27.cloned.1.call-done = f32[256,768]{1,0:T(8,128)} async-done(((f32[1024,768]{1,0:T(8,128)}), f32[256,768]{1,0:T(8,128)}) %reduce-scatter.27.cloned.1.call-update) | async-done | bytes 786448 | tf_op jit(solution)/shard_map/reduce_scatter | solution.py:373
  839.0 19.8 %all-gather.31.cloned.1.call-done = bf16[1024,768]{1,0:T(8,128)(2,1)} async-done(((bf16[256,768]{1,0:T(8,128)(2,1)}), bf16[1024,768]{1,0:T(8,128)(2,1)}) %all-gather.31.cloned.1.call-update) | async-done | bytes 1572880 | tf_op jit(solution)/shard_map/all_gather | solution.py:294
  867.6 38.0 %reduce-scatter.33.cloned.1.call-done = f32[256,768]{1,0:T(8,128)} async-done(((f32[1024,768]{1,0:T(8,128)}), f32[256,768]{1,0:T(8,128)}) %reduce-scatter.33.cloned.1.call-update) | async-done | bytes 786448 | tf_op jit(solution)/shard_map/reduce_scatter | solution.py:299
  934.4 55.1 %while.79 = (s32[]{:T(128)}, f32[1024,3,64]{0,2,1:T(8,128)}, f32[1024,3,64]{0,2,1:T(8,128)}, bf16[2,512,3,64]{1,3,2,0:T(8,128)(2,1)}, s32[2]{0:T(128)}, /*index=...) while((s32[]{:T(128)}, f32[1024,3,64]{0,2,1:T(8,128)}, ...), condition=%wide.region_58.59_spmd.clone, body=%wide.region_56.58_spmd.clone.sunk | while | flops 1031928320 | bytes 85580312 | solution.py:103
  1016.1 116.5 %all-reduce.3.cloned.1.call-done = (f32[1,2,768,8]{2,3,1,0:T(8,128)}, f32[1,2,768,8]{2,3,1,0:T(8,128)}, f32[1,2,8,768]{3,2,1,0:T(8,128)}, f32[1,2,8,768]{3,2,1,0:T(8,128)}) async-done(((f32[1,2,768,8]{2,3,1,0:T(8,128)}, f32[1,2,768,8]{2,3,1,0:T(8,128)}, f32[1,2,8,768]{3,2,1,0:T(8,128)}, f32[1,2,8,768]{3,2,1,0:T(8,128)}), (f32[1,2,768,8]{2,3,1,0:T(8,128)}, f32[1,2,768,8]{2,3,1,0:T(8,128)}, ...) | async-done | bytes 196624 | tf_op jit(solution)/shard_map/psum | solution.py:396
  1135.5 38.7 %reduce-scatter.35.cloned.1.call-done = f32[256,768]{1,0:T(8,128)} async-done(((f32[1024,768]{1,0:T(8,128)}), f32[256,768]{1,0:T(8,128)}) %reduce-scatter.35.cloned.1.call-update) | async-done | bytes 786448 | tf_op jit(solution)/shard_map/reduce_scatter | solution.py:373
  (569 shorter events, 463.5 us)
Async XLA Ops:
  7.2 75.5 %all-gather.15.cloned.1.call-start = ((), (), s32[]{:S(2)}) async-start(), calls=%async_computation.12 | async-start | bytes 1966080 | tf_op jit(solution)/shard_map/all_gather | solution.py:187
  7.9 144.5 %reduce-scatter.13.cloned.1.call-start = ((), (), s32[]{:S(2)}) async-start(), calls=%async_computation.13 | async-start | bytes 3932160 | tf_op jit(solution)/shard_map/reduce_scatter | solution.py:209
  113.7 79.4 %reduce-scatter.29.cloned.1.call-start = ((), (), s32[]{:S(2)}) async-start(), calls=%async_computation.27 | async-start | bytes 3932160 | tf_op jit(solution)/shard_map/reduce_scatter | solution.py:209
  131.5 84.7 %all-gather.29.cloned.1.call-start = ((), (), s32[]{:S(2)}) async-start(), calls=%async_computation.28 | async-start | bytes 1966080 | tf_op jit(solution)/shard_map/all_gather | solution.py:225
  132.2 186.8 %copy-start.71 = (f32[768]{0:T(1024)}, f32[768]{0:T(1024)S(1)}, u32[]{:S(2)}) copy-start(f32[768]{0:T(1024)S(1)} %get-tuple-element.380) | copy-start | bytes 9220
  196.5 41.5 %all-gather.17.cloned.1.call-start = ((), (), s32[]{:S(2)}) async-start(), calls=%async_computation.14 | async-start | bytes 1966080 | tf_op jit(solution)/shard_map/all_gather | solution.py:225
  197.2 81.1 %reduce-scatter.31.cloned.1.call-start = ((), (), s32[]{:S(2)}) async-start(), calls=%async_computation.29 | async-start | bytes 3932160 | tf_op jit(solution)/shard_map/reduce_scatter | solution.py:233
  231.8 87.2 %reduce-scatter.15.cloned.1.call-start = ((), (), s32[]{:S(2)}) async-start(), calls=%async_computation.15 | async-start | bytes 3932160 | tf_op jit(solution)/shard_map/reduce_scatter | solution.py:233
  250.5 140.3 %all-gather.19.cloned.1.call-start = ((), (), s32[]{:S(2)}) async-start(), calls=%async_computation.16 | async-start | bytes 1966080 | tf_op jit(solution)/shard_map/all_gather | solution.py:187
  323.6 139.5 %reduce-scatter.17.cloned.1.call-start = ((), (), s32[]{:S(2)}) async-start(), calls=%async_computation.17 | async-start | bytes 3932160 | tf_op jit(solution)/shard_map/reduce_scatter | solution.py:209
  425.2 78.4 %reduce-scatter.21.cloned.1.call-start = ((), (), s32[]{:S(2)}) async-start(), calls=%async_computation.20 | async-start | bytes 3932160 | tf_op jit(solution)/shard_map/reduce_scatter | solution.py:209
  442.4 85.9 %all-gather.23.cloned.1.call-start = ((), (), s32[]{:S(2)}) async-start(), calls=%async_computation.21 | async-start | bytes 1966080 | tf_op jit(solution)/shard_map/all_gather | solution.py:225
  508.5 41.5 %all-gather.21.cloned.1.call-start = ((), (), s32[]{:S(2)}) async-start(), calls=%async_computation.18 | async-start | bytes 1966080 | tf_op jit(solution)/shard_map/all_gather | solution.py:225
  509.1 81.4 %reduce-scatter.23.cloned.1.call-start = ((), (), s32[]{:S(2)}) async-start(), calls=%async_computation.22 | async-start | bytes 3932160 | tf_op jit(solution)/shard_map/reduce_scatter | solution.py:233
  543.8 87.2 %reduce-scatter.19.cloned.1.call-start = ((), (), s32[]{:S(2)}) async-start(), calls=%async_computation.19 | async-start | bytes 3932160 | tf_op jit(solution)/shard_map/reduce_scatter | solution.py:233
  562.5 93.2 %all-gather.25.cloned.1.call-start = ((), (), s32[]{:S(2)}) async-start(), calls=%async_computation.23 | async-start | bytes 1966080 | tf_op jit(solution)/shard_map/all_gather | solution.py:294
  635.9 66.6 %reduce-scatter.25.cloned.1.call-start = ((), (), s32[]{:S(2)}) async-start(), calls=%async_computation.24 | async-start | bytes 3932160 | tf_op jit(solution)/shard_map/reduce_scatter | solution.py:299
  664.5 62.0 %all-gather.27.cloned.1.call-start = ((), (), s32[]{:S(2)}) async-start(), calls=%async_computation.25 | async-start | bytes 1966080 | tf_op jit(solution)/shard_map/all_gather | solution.py:306
  706.6 128.4 %reduce-scatter.27.cloned.1.call-start = ((), (), s32[]{:S(2)}) async-start(), calls=%async_computation.26 | async-start | bytes 3932160 | tf_op jit(solution)/shard_map/reduce_scatter | solution.py:373
  796.9 61.9 %all-gather.31.cloned.1.call-start = ((), (), s32[]{:S(2)}) async-start(), calls=%async_computation.30 | async-start | bytes 1966080 | tf_op jit(solution)/shard_map/all_gather | solution.py:294
  839.0 66.6 %reduce-scatter.33.cloned.1.call-start = ((), (), s32[]{:S(2)}) async-start(), calls=%async_computation.31 | async-start | bytes 3932160 | tf_op jit(solution)/shard_map/reduce_scatter | solution.py:299
  867.5 63.5 %all-gather.33.cloned.1.call-start = ((), (), s32[]{:S(2)}) async-start(), calls=%async_computation.32 | async-start | bytes 1966080 | tf_op jit(solution)/shard_map/all_gather | solution.py:306
  911.2 221.4 %all-reduce.3.cloned.1.call-start = ((), (), s32[]{:S(2)}) async-start(), calls=%async_computation.34 | async-start | bytes 393216 | tf_op jit(solution)/shard_map/psum | solution.py:396
  1007.8 166.4 %reduce-scatter.35.cloned.1.call-start = ((), (), s32[]{:S(2)}) async-start(), calls=%async_computation.33 | async-start | bytes 3932160 | tf_op jit(solution)/shard_map/reduce_scatter | solution.py:373
  (133 other events, 2752.4 us)
Sparse Core Ops, SparseCore 0:
  9.6 22.3 all-gather.14
  113.8 38.5 reduce-scatter.12
  155.1 37.9 reduce-scatter.28
  196.6 19.6 all-gather.28
  218.3 19.6 all-gather.16
  240.3 37.9 reduce-scatter.30
  281.0 37.9 reduce-scatter.14
  323.8 19.6 all-gather.18
  425.3 37.7 reduce-scatter.16
  465.6 37.9 reduce-scatter.20
  508.6 19.6 all-gather.22
  530.3 19.6 all-gather.20
  552.5 37.9 reduce-scatter.22
  593.0 37.9 reduce-scatter.18
  636.0 19.6 all-gather.24
  664.6 37.9 reduce-scatter.24
  706.7 19.6 all-gather.26
  797.0 37.9 reduce-scatter.26
  839.1 19.6 all-gather.30
  867.6 37.9 reduce-scatter.32
  911.3 19.6 all-gather.32
  1008.0 124.5 all-reduce.2
  1135.3 38.8 reduce-scatter.34
where the time goes:
time: 1190 us; the launch traced here: 1180 us
  waiting for transfers between devices  649 us (55%)
  matrix products  259 us (22%)
  blocking collectives  133 us (11%)
  other arithmetic  65.4 us (5%)
  local copies, waits for them, and re-layouts  42.1 us (4%)
  loops' own time  16.6 us (1%)
  between operations  15.8 us (1%)
    reduce_scatter x4, waiting for transfers between devices, layer_forward(): lax.psum_scatter(jnp.dot(piece_rows, out_full, preferred_element_type=jnp...  137 us
    reduce_scatter x4, waiting for transfers between devices, layer_forward(): lax.psum_scatter(jnp.einsum('rc,dc->rd', piece_rows, out_proj, preferred_...  118 us
    psum x1, waiting for transfers between devices, body(): grad_a, grad_b = lax.psum((grad_a, grad_b), ('dp', 'tensor'))  117 us
    reduce_scatter x2, waiting for transfers between devices, layer_backward(): lax.psum_scatter(term_sum, 'tensor', scatter_dimension=0, tiled=True)  76.2 us
    reduce_scatter x2, waiting for transfers between devices, layer_backward(): lax.psum_scatter(jnp.einsum('rf,df->rd', grad_pre, in_full, preferred_ele...  76.1 us
    all_gather x2, blocking collectives, frozen_weights(): lax.all_gather(query_key_value_weight[current_layer_index], 'dp', axis=1,...  68.6 us
    all_gather x2, blocking collectives, frozen_weights(): lax.all_gather(output_projection_weight[current_layer_index], 'dp', axis=...  64.1 us
    all_gather x4, waiting for transfers between devices, layer_forward(): lax.all_gather(normed_low, 'tensor', axis=0, tiled=True)  50.1 us
  transfers between devices with their start and end apart: 23, of which 21 were waited for; matrix products, arithmetic and copies ran while one was open for 9% of the time, Pallas kernels for 0%

commit v1 on v0

v1 whole, which is shorter than its diff:
```python
import functools

import jax
import jax.numpy as jnp
from jax import lax
from jax.experimental import pallas as pl
from jax.experimental.pallas import tpu as pltpu
from jax.sharding import PartitionSpec as P

MODEL_WIDTH = 768
HEAD_DIM = 64
ADAPTER_RANK = 8
ENCODER_LAYERS = 2
SET_HEADS = 6
SET_COLS = SET_HEADS * HEAD_DIM
KEY_BLOCK = 128
EPSILON = 1e-05
MASKED = -1000000000.0
VMEM_LIMIT = 56 * 1024 * 1024

F32 = jnp.float32
BF16 = jnp.bfloat16


def dot_nn(a, b):
    return lax.dot_general(a, b, (((1,), (0,)), ((), ())), preferred_element_type=F32)


def dot_nt(a, b):
    return lax.dot_general(a, b, (((1,), (1,)), ((), ())), preferred_element_type=F32)


def dot_tn(a, b):
    return lax.dot_general(a, b, (((0,), (0,)), ((), ())), preferred_element_type=F32)


def aligned(start, size):
    return pl.ds(pl.multiple_of(start, size), size)


def range_of_rows(meta_ref, slots, first_row, rows, group_len):
    row = first_row + lax.broadcasted_iota(jnp.int32, (1, rows), 1)
    start = jnp.zeros((1, rows), jnp.int32)
    end = jnp.full((1, rows), group_len, jnp.int32)
    for s in range(slots):
        e = meta_ref[s]
        start = jnp.where(e <= row, jnp.maximum(start, e), start)
        end = jnp.where(e > row, jnp.minimum(end, e), end)
    return start, end


def scalar_range(meta_ref, slots, first_row, last_row, group_len):
    low = jnp.int32(0)
    high = jnp.int32(group_len)
    for s in range(slots):
        e = meta_ref[s]
        low = jnp.where(e <= first_row, jnp.maximum(low, e), low)
        high = jnp.where(e > last_row, jnp.minimum(high, e), high)
    return low, high


def piece_copies(pieces, source_of, target_of, sem, shard):
    out = []
    rows = MODEL_WIDTH // len(pieces)
    for k, piece in enumerate(pieces):
        if len(pieces) == 1:
            target = target_of(pl.ds(0, rows))
        else:
            target = target_of(aligned(jnp.bitwise_xor(shard, k) * rows, rows))
        out.append(pltpu.make_async_copy(source_of(piece), target, sem))
    return out


def attention_forward_kernel(n_pieces, slots, group_len, meta, *refs):
    x_refs = refs[:4]
    pieces = refs[4 : 4 + n_pieces]
    adapter, up, bias = refs[4 + n_pieces : 7 + n_pieces]
    q_out, k_out, v_out, lse_out, c_out, own_out, sib_out = refs[7 + n_pieces : 14 + n_pieces]
    xs, w, qm, down, vt, acc, x_sem, w_sem = refs[14 + n_pieces :]
    rows_dev = x_refs[0].shape[0]
    chip_rows = 2 * rows_dev
    t = meta[slots]
    shard = meta[slots + 1]
    core = jnp.bitwise_and(t, 1)
    chip0 = (t - core) * rows_dev

    x_copies = [
        pltpu.make_async_copy(
            x_refs[j], xs.at[aligned(jnp.bitwise_xor(t, j) * rows_dev, rows_dev)], x_sem.at[j]
        )
        for j in range(4)
    ]
    for c in x_copies:
        c.start()
    w_copies = [
        piece_copies(pieces, lambda p, m=m: p.at[m], lambda r, m=m: w.at[m, r], w_sem.at[m], shard)
        for m in range(4)
    ]
    for group in w_copies:
        for c in group:
            c.start()
    low, high = scalar_range(meta, slots, chip0, chip0 + chip_rows - 1, group_len)
    for c in x_copies:
        c.wait()
    for m in (1, 2):
        for c in w_copies[m]:
            c.wait()

    def project_block(b, _):
        rows = aligned(b * rows_dev, rows_dev)
        xb = xs[rows]
        db = dot_nn(xb, adapter[...]).astype(BF16)
        down[rows] = db
        k_out[rows] = dot_nn(xb, w[1]).astype(BF16)
        vb = (dot_nn(xb, w[2]) + dot_nn(db, up[1]) + bias[1:2]).astype(BF16)
        v_out[rows] = vb
        vb_t = vb.T
        for half in range(rows_dev // KEY_BLOCK):
            vt[b * (rows_dev // KEY_BLOCK) + half] = vb_t[:, half * KEY_BLOCK : (half + 1) * KEY_BLOCK]
        return 0

    lax.fori_loop(low // rows_dev, (high + rows_dev - 1) // rows_dev, project_block, 0)

    for c in w_copies[0]:
        c.wait()
    lane = lax.broadcasted_iota(jnp.int32, (rows_dev, 128), 1)
    for qb in range(2):
        rows = aligned(chip0 + qb * rows_dev, rows_dev)
        here = pl.ds(qb * rows_dev, rows_dev)
        qv = (dot_nn(xs[rows], w[0]) + dot_nn(down[rows], up[0]) + bias[0:1]) * HEAD_DIM**-0.5
        qv = qv.astype(BF16)
        q_out[here] = qv
        for h in range(SET_HEADS):
            pair = qv[:, (h // 2) * 128 : (h // 2 + 1) * 128]
            keep = (lane < HEAD_DIM) if h % 2 == 0 else (lane >= HEAD_DIM)
            qm[h] = jnp.where(keep, pair, jnp.zeros_like(pair))

        first = chip0 + qb * rows_dev
        klow, khigh = scalar_range(meta, slots, first, first + rows_dev - 1, group_len)
        q_start, q_end = range_of_rows(meta, slots, first, rows_dev, group_len)
        acc[...] = jnp.zeros_like(acc)

        def key_step(kb, carry, q_start=q_start, q_end=q_end):
            tops, sums = carry
            keys = aligned(kb * KEY_BLOCK, KEY_BLOCK)
            kpos = kb * KEY_BLOCK + lax.broadcasted_iota(jnp.int32, (KEY_BLOCK, rows_dev), 0)
            mask = jnp.where((kpos >= q_start) & (kpos < q_end), 0.0, MASKED)
            new_tops, new_sums = [], []
            for h in range(SET_HEADS):
                s = dot_nt(k_out[keys, (h // 2) * 128 : (h // 2 + 1) * 128], qm[h]) + mask
                top = jnp.maximum(tops[h], jnp.max(s, axis=0, keepdims=True))
                p = jnp.exp(s - top)
                fade = jnp.exp(tops[h] - top)
                new_tops.append(top)
                new_sums.append(sums[h] * fade + jnp.sum(p, axis=0, keepdims=True))
                cols = pl.ds(h * HEAD_DIM, HEAD_DIM)
                acc[cols] = acc[cols] * fade + dot_nn(
                    vt[kb, h * HEAD_DIM : (h + 1) * HEAD_DIM, :], p.astype(BF16)
                )
            return tuple(new_tops), tuple(new_sums)

        init = (
            tuple(jnp.full((1, rows_dev), -3e38, F32) for _ in range(SET_HEADS)),
            tuple(jnp.zeros((1, rows_dev), F32) for _ in range(SET_HEADS)),
        )
        tops, sums = lax.fori_loop(
            klow // KEY_BLOCK, (khigh + KEY_BLOCK - 1) // KEY_BLOCK, key_step, init
        )
        for h in range(SET_HEADS):
            cols = pl.ds(h * HEAD_DIM, HEAD_DIM)
            acc[cols] = acc[cols] / sums[h]
            lse_out[h : h + 1, qb * rows_dev : (qb + 1) * rows_dev] = tops[h] + jnp.log(sums[h])
        c_out[here] = acc[...].T.astype(BF16)

    for c in w_copies[3]:
        c.wait()
    own_out[...] = dot_nt(c_out[aligned(core * rows_dev, rows_dev)], w[3])
    sib_out[...] = dot_nt(c_out[aligned((1 - core) * rows_dev, rows_dev)], w[3]).astype(BF16)


ANY = pl.BlockSpec(memory_space=pl.ANY)
SMEM = pl.BlockSpec(memory_space=pltpu.SMEM)
VMEM = pl.BlockSpec(memory_space=pltpu.VMEM)


def estimate(flops, nbytes):
    return pl.CostEstimate(flops=flops, bytes_accessed=nbytes, transcendentals=0)


def attention_forward(meta, xs, pieces, adapter, up, bias):
    rows = xs[0].shape[0]
    group = 4 * rows
    slots = meta.shape[0] - 2
    n = len(pieces)
    return pl.pallas_call(
        functools.partial(attention_forward_kernel, n, slots, group),
        out_shape=(
            jax.ShapeDtypeStruct((2 * rows, SET_COLS), BF16),
            jax.ShapeDtypeStruct((group, SET_COLS), BF16),
            jax.ShapeDtypeStruct((group, SET_COLS), BF16),
            jax.ShapeDtypeStruct((8, 2 * rows), F32),
            jax.ShapeDtypeStruct((2 * rows, SET_COLS), BF16),
            jax.ShapeDtypeStruct((rows, MODEL_WIDTH), F32),
            jax.ShapeDtypeStruct((rows, MODEL_WIDTH), BF16),
        ),
        in_specs=[SMEM] + [ANY] * (4 + n) + [VMEM] * 3,
        out_specs=[VMEM] * 7,
        scratch_shapes=[
            pltpu.VMEM((group, MODEL_WIDTH), BF16),
            pltpu.VMEM((4, MODEL_WIDTH, SET_COLS), BF16),
            pltpu.VMEM((SET_HEADS, rows, 128), BF16),
            pltpu.VMEM((group, 128), BF16),
            pltpu.VMEM((group // KEY_BLOCK, SET_COLS, KEY_BLOCK), BF16),
            pltpu.VMEM((SET_COLS, rows), F32),
            pltpu.SemaphoreType.DMA((4,)),
            pltpu.SemaphoreType.DMA((4,)),
        ],
        compiler_params=pltpu.CompilerParams(vmem_limit_bytes=VMEM_LIMIT),
        cost_estimate=estimate(6_000_000_000, 8_000_000),
        name="attention_forward",
    )(meta, *xs, *pieces, adapter, up, bias)


def attention_backward_kernel(n_pieces, slots, group_len, meta, *refs):
    x_refs = refs[:4]
    pieces = refs[4 : 4 + n_pieces]
    g_low, g_sib, g_own, q_in, k_in, v_in, lse, c_in, adapter, up = refs[4 + n_pieces : 14 + n_pieces]
    out0, out1, out2, out3, grads = refs[14 + n_pieces : 19 + n_pieces]
    xs, w, gl, gc, gcm, qm, kt, gk, gv, gqt, down, ga, gb, x_sem, w_sem = refs[19 + n_pieces :]
    rows_dev = x_refs[0].shape[0]
    chip_rows = 2 * rows_dev
    t = meta[slots]
    shard = meta[slots + 1]
    core = jnp.bitwise_and(t, 1)
    chip0 = (t - core) * rows_dev
    w_copies = [
        piece_copies(pieces, lambda p, m=m: p.at[m], lambda r, m=m: w.at[m, r], w_sem.at[m], shard)
        for m in range(4)
    ]
    for m in (3, 0, 1, 2):
        for c in w_copies[m]:
            c.start()
    x_copies = [
        pltpu.make_async_copy(
            x_refs[j], xs.at[aligned(jnp.bitwise_xor(t, j) * rows_dev, rows_dev)], x_sem.at[j]
        )
        for j in range(4)
    ]
    for c in x_copies:
        c.start()
    low, high = scalar_range(meta, slots, chip0, chip0 + chip_rows - 1, group_len)
    block_low = low // rows_dev
    block_high = (high + rows_dev - 1) // rows_dev

    gl[aligned(core * rows_dev, rows_dev)] = g_low[...]
    gl[aligned((1 - core) * rows_dev, rows_dev)] = g_sib[...]
    for c in w_copies[3]:
        c.wait()
    gc[...] = dot_nn(gl[...], w[3]).astype(BF16)
    for c in x_copies:
        c.wait()

    def prepare_block(b, _):
        rows = aligned(b * rows_dev, rows_dev)
        down[rows] = dot_nn(xs[rows], adapter[...]).astype(BF16)
        kb_t = k_in[rows].T
        for half in range(rows_dev // KEY_BLOCK):
            kt[b * (rows_dev // KEY_BLOCK) + half] = kb_t[:, half * KEY_BLOCK : (half + 1) * KEY_BLOCK]
        gk[rows] = jnp.zeros((rows_dev, SET_COLS), F32)
        gv[rows] = jnp.zeros((rows_dev, SET_COLS), F32)
        return 0

    lax.fori_loop(block_low, block_high, prepare_block, 0)

    pick = (
        lax.broadcasted_iota(jnp.int32, (8, SET_COLS), 1) // HEAD_DIM
        == lax.broadcasted_iota(jnp.int32, (8, SET_COLS), 0)
    ).astype(BF16)
    lane = lax.broadcasted_iota(jnp.int32, (rows_dev, 128), 1)
    for qb in range(2):
        here = pl.ds(qb * rows_dev, rows_dev)
        cols_here = slice(qb * rows_dev, (qb + 1) * rows_dev)
        product = gc[here].astype(F32) * c_in[here].astype(F32)
        product_high = product.astype(BF16)
        product_low = (product - product_high.astype(F32)).astype(BF16)
        delta = dot_nt(pick, product_high) + dot_nt(pick, product_low)
        for h in range(SET_HEADS):
            cols = slice((h // 2) * 128, (h // 2 + 1) * 128)
            keep = (lane < HEAD_DIM) if h % 2 == 0 else (lane >= HEAD_DIM)
            pair = q_in[here, cols]
            qm[h] = jnp.where(keep, pair, jnp.zeros_like(pair))
            pair = gc[here, cols]
            gcm[h] = jnp.where(keep, pair, jnp.zeros_like(pair))
        first = chip0 + qb * rows_dev
        klow, khigh = scalar_range(meta, slots, first, first + rows_dev - 1, group_len)
        q_start, q_end = range_of_rows(meta, slots, first, rows_dev, group_len)
        gqt[...] = jnp.zeros_like(gqt)

        def key_step(kb, _, q_start=q_start, q_end=q_end, delta=delta, cols_here=cols_here):
            keys = aligned(kb * KEY_BLOCK, KEY_BLOCK)
            kpos = kb * KEY_BLOCK + lax.broadcasted_iota(jnp.int32, (KEY_BLOCK, rows_dev), 0)
            mask = jnp.where((kpos >= q_start) & (kpos < q_end), 0.0, MASKED)
            for pair in range(SET_HEADS // 2):
                cols = slice(pair * 128, (pair + 1) * 128)
                kp = k_in[keys, cols]
                vp = v_in[keys, cols]
                gk_sum = gk[keys, cols]
                gv_sum = gv[keys, cols]
                for h in (2 * pair, 2 * pair + 1):
                    s = dot_nt(kp, qm[h]) + mask
                    p = jnp.exp(s - lse[h : h + 1, cols_here])
                    gp = dot_nt(vp, gcm[h])
                    gs = (p * (gp - delta[h : h + 1])).astype(BF16)
                    head = slice(h * HEAD_DIM, (h + 1) * HEAD_DIM)
                    gqt[head] += dot_nn(kt[kb, head, :], gs)
                    gk_sum = gk_sum + dot_nn(gs, qm[h])
                    gv_sum = gv_sum + dot_nn(p.astype(BF16), gcm[h])
                gk[keys, cols] = gk_sum
                gv[keys, cols] = gv_sum
            return 0

        lax.fori_loop(klow // KEY_BLOCK, (khigh + KEY_BLOCK - 1) // KEY_BLOCK, key_step, 0)
        gc[here] = (gqt[...].T * HEAD_DIM**-0.5).astype(BF16)

    for m in (0, 1, 2):
        for c in w_copies[m]:
            c.wait()
    ga[...] = jnp.zeros_like(ga)
    gb[...] = jnp.zeros_like(gb)

    def input_gradient(b):
        rows = aligned(b * rows_dev, rows_dev)
        gvb = gv[rows].astype(BF16)
        gd = dot_nt(gvb, up[1])
        g = dot_nt(gk[rows].astype(BF16), w[1]) + dot_nt(gvb, w[2])
        gb[1] += dot_tn(down[rows], gvb)
        return g, gd

    def query_gradient(b):
        gq = gc[aligned(b * rows_dev - chip0, rows_dev)]
        gd = dot_nt(gq, up[0])
        g = dot_nt(gq, w[0])
        gb[0] += dot_tn(down[aligned(b * rows_dev, rows_dev)], gq)
        return g, gd

    def add_adapter(b, g, gd):
        gd = gd.astype(BF16)
        ga[...] += dot_tn(gd, xs[aligned(b * rows_dev, rows_dev)])
        return g + dot_nt(gd, adapter[...])

    for j, out in ((2, out2), (3, out3)):
        b = jnp.bitwise_xor(t, j)
        used = (b >= block_low) & (b < block_high)

        @pl.when(used)
        def _(b=b, out=out):
            g, gd = input_gradient(b)
            out[...] = add_adapter(b, g, gd).astype(BF16)

        @pl.when(jnp.logical_not(used))
        def _(out=out):
            out[...] = jnp.zeros_like(out)

    for j, out in ((1, out1), (0, out0)):
        b = jnp.bitwise_xor(t, j)
        g, gd = input_gradient(b)
        gq, gdq = query_gradient(b)
        g = add_adapter(b, g + gq, gd + gdq)
        out[...] = (g + g_own[...] if j == 0 else g).astype(out.dtype)

    grads[0:16] = ga[0:16]
    for c in range(2):
        cols = slice(c * SET_COLS, (c + 1) * SET_COLS)
        mine = jnp.where(core == c, 2.0, 0.0)
        grads[16:24, cols] = gb[0, 0:8] * mine
        grads[24:32, cols] = gb[1, 8:16] * mine


def attention_backward(meta, xs, pieces, g_low, g_sib, g_own, saved, adapter, up):
    rows = xs[0].shape[0]
    group = 4 * rows
    slots = meta.shape[0] - 2
    n = len(pieces)
    block = jax.ShapeDtypeStruct((rows, MODEL_WIDTH), BF16)
    return pl.pallas_call(
        functools.partial(attention_backward_kernel, n, slots, group),
        out_shape=(
            jax.ShapeDtypeStruct((rows, MODEL_WIDTH), F32),
            block,
            block,
            block,
            jax.ShapeDtypeStruct((32, MODEL_WIDTH), F32),
        ),
        in_specs=[SMEM] + [ANY] * (4 + n) + [VMEM] * 10,
        out_specs=[VMEM] * 5,
        scratch_shapes=[
            pltpu.VMEM((group, MODEL_WIDTH), BF16),
            pltpu.VMEM((4, MODEL_WIDTH, SET_COLS), BF16),
            pltpu.VMEM((2 * rows, MODEL_WIDTH), BF16),
            pltpu.VMEM((2 * rows, SET_COLS), BF16),
            pltpu.VMEM((SET_HEADS, rows, 128), BF16),
            pltpu.VMEM((SET_HEADS, rows, 128), BF16),
            pltpu.VMEM((group // KEY_BLOCK, SET_COLS, KEY_BLOCK), BF16),
            pltpu.VMEM((group, SET_COLS), F32),
            pltpu.VMEM((group, SET_COLS), F32),
            pltpu.VMEM((SET_COLS, rows), F32),
            pltpu.VMEM((group, 128), BF16),
            pltpu.VMEM((128, MODEL_WIDTH), F32),
            pltpu.VMEM((2, 128, SET_COLS), F32),
            pltpu.SemaphoreType.DMA((4,)),
            pltpu.SemaphoreType.DMA((4,)),
        ],
        compiler_params=pltpu.CompilerParams(vmem_limit_bytes=VMEM_LIMIT),
        cost_estimate=estimate(10_000_000_000, 8_000_000),
        name="attention_backward",
    )(meta, *xs, *pieces, g_low, g_sib, g_own, *saved, adapter, up)


def norm_parts(v):
    mean = jnp.mean(v, axis=-1, keepdims=True)
    centered = v - mean
    rstd = lax.rsqrt(jnp.mean(centered * centered, axis=-1, keepdims=True) + EPSILON)
    return centered * rstd, rstd


def norm_back(g, gain, n, rstd):
    q = g * gain
    return rstd * (
        q - jnp.mean(q, axis=-1, keepdims=True) - n * jnp.mean(q * n, axis=-1, keepdims=True)
    )


def normal_cdf(u):
    z = jnp.abs(u) * 0.7071067811865476
    s = 1.0 / (1.0 + 0.3275911 * z)
    poly = s * (
        0.254829592
        + s * (-0.284496736 + s * (1.421413741 + s * (-1.453152027 + s * 1.061405429)))
    )
    e = jnp.exp(-z * z)
    tail = 0.5 * poly * e
    return jnp.where(u >= 0.0, 1.0 - tail, tail), e * 0.3989422804014327


def split_refs(refs, counts):
    out = []
    for n in counts:
        out.append(refs[:n])
        refs = refs[n:]
    return out, refs


def start_weights(groups, w, sem, shard):
    copies = [
        piece_copies(pieces, lambda p: p, lambda r, m=m: w.at[m, r], sem.at[m], shard)
        for m, pieces in enumerate(groups)
    ]
    for group in copies:
        for c in group:
            c.start()
    return copies


def feedforward_forward_kernel(counts, slots, meta, *refs):
    x, own, sib, vecs, ff_bias = refs[:5]
    groups, refs = split_refs(refs[5:], counts)
    f1_out, f2_out, slope_out, z_out, w, hid, y_scr, sem = refs
    copies = start_weights(groups, w, sem, meta[slots + 1])
    f1 = x[...].astype(F32) + own[...] + sib[...].astype(F32) + vecs[0:1]
    f1_out[...] = f1
    n, _ = norm_parts(f1)
    y = n * vecs[4:5] + vecs[1:2]
    y_scr[...] = y
    y_low = y.astype(BF16)
    rows = x.shape[0]
    for j in range(4):
        for c in copies[2 * j]:
            c.wait()
        for part in range(3):
            cols = slice(part * 256, (part + 1) * 256)
            u = dot_nn(y_low, w[2 * j, :, cols]) + ff_bias[j : j + 1, cols]
            cdf, density = normal_cdf(u)
            hid[j, :, cols] = (u * cdf).astype(BF16)
            slope_out[j, :, cols] = (cdf + u * density).astype(BF16)
    f2 = y_scr[...] + vecs[2:3]
    for j in range(4):
        for c in copies[2 * j + 1]:
            c.wait()
        f2 = f2 + dot_nn(hid[j], w[2 * j + 1])
    f2_out[...] = f2
    n2, _ = norm_parts(f2)
    z_out[...] = (n2 * vecs[5:6] + vecs[3:4]).astype(BF16)


def feedforward_forward(meta, x, own, sib, vecs, ff_bias, groups):
    rows = x.shape[0]
    slots = meta.shape[0] - 2
    counts = [len(g) for g in groups]
    flat = [p for g in groups for p in g]
    wide = jax.ShapeDtypeStruct((rows, MODEL_WIDTH), F32)
    return pl.pallas_call(
        functools.partial(feedforward_forward_kernel, counts, slots),
        out_shape=(
            wide,
            wide,
            jax.ShapeDtypeStruct((4, rows, MODEL_WIDTH), BF16),
            jax.ShapeDtypeStruct((rows, MODEL_WIDTH), BF16),
        ),
        in_specs=[SMEM] + [VMEM] * 5 + [ANY] * len(flat),
        out_specs=[VMEM] * 4,
        scratch_shapes=[
            pltpu.VMEM((8, MODEL_WIDTH, MODEL_WIDTH), BF16),
            pltpu.VMEM((4, rows, MODEL_WIDTH), BF16),
            pltpu.VMEM((rows, MODEL_WIDTH), F32),
            pltpu.SemaphoreType.DMA((8,)),
        ],
        compiler_params=pltpu.CompilerParams(vmem_limit_bytes=VMEM_LIMIT),
        cost_estimate=estimate(6_000_000_000, 12_000_000),
        name="feedforward_forward",
    )(meta, x, own, sib, vecs, ff_bias, *flat)


def feedforward_backward_kernel(counts, slots, n_g, meta, *refs):
    g_refs = refs[:n_g]
    f1, f2, slope, vecs = refs[n_g : n_g + 4]
    groups, refs = split_refs(refs[n_g + 4 :], counts)
    g_out, low_out, w, gu, sem = refs
    copies = start_weights(groups, w, sem, meta[slots + 1])
    g = g_refs[0][...].astype(F32)
    for r in g_refs[1:]:
        g = g + r[...].astype(F32)
    n2, r2 = norm_parts(f2[...])
    gf2 = norm_back(g, vecs[5:6], n2, r2)
    g_out[...] = gf2
    gf2_low = gf2.astype(BF16)
    for j in range(4):
        for c in copies[2 * j + 1]:
            c.wait()
        for part in range(3):
            cols = slice(part * 256, (part + 1) * 256)
            gh = dot_nt(gf2_low, w[2 * j + 1, cols, :])
            gu[j, :, cols] = (gh * slope[j, :, cols].astype(F32)).astype(BF16)
    gy = g_out[...]
    for j in range(4):
        for c in copies[2 * j]:
            c.wait()
        gy = gy + dot_nt(gu[j], w[2 * j])
    n1, r1 = norm_parts(f1[...])
    gf1 = norm_back(gy, vecs[4:5], n1, r1)
    g_out[...] = gf1
    low_out[...] = gf1.astype(BF16)


def feedforward_backward(meta, gs, f1, f2, slope, vecs, groups):
    rows = f1.shape[0]
    slots = meta.shape[0] - 2
    counts = [len(g) for g in groups]
    flat = [p for g in groups for p in g]
    return pl.pallas_call(
        functools.partial(feedforward_backward_kernel, counts, slots, len(gs)),
        out_shape=(
            jax.ShapeDtypeStruct((rows, MODEL_WIDTH), F32),
            jax.ShapeDtypeStruct((rows, MODEL_WIDTH), BF16),
        ),
        in_specs=[SMEM] + [VMEM] * (len(gs) + 4) + [ANY] * len(flat),
        out_specs=[VMEM] * 2,
        scratch_shapes=[
            pltpu.VMEM((8, MODEL_WIDTH, MODEL_WIDTH), BF16),
            pltpu.VMEM((4, rows, MODEL_WIDTH), BF16),
            pltpu.SemaphoreType.DMA((8,)),
        ],
        compiler_params=pltpu.CompilerParams(vmem_limit_bytes=VMEM_LIMIT),
        cost_estimate=estimate(6_000_000_000, 12_000_000),
        name="feedforward_backward",
    )(meta, *gs, f1, f2, slope, vecs, *flat)


def swap(value, axis, flip):
    size = lax.axis_size(axis)
    return lax.ppermute(value, axis, [(i, i ^ flip) for i in range(size)])


def gather_pieces(piece):
    size = lax.axis_size("dp")
    got = {0: piece}
    got[1] = swap(piece, "dp", 1)
    for k in range(2, size, 2):
        got[k] = swap(piece, "dp", k)
    for k in range(2, size, 2):
        got[k + 1] = swap(got[k], "dp", 1)
    return [got[k] for k in range(size)]


def sum_all(value):
    for axis in ("tensor", "dp"):
        size = lax.axis_size(axis)
        flip = 1
        while flip < size:
            value = value + swap(value, axis, flip)
            flip *= 2
    return value


def set_columns(value):
    def part(device, first, last):
        return value[..., device * 192 + first : device * 192 + last]

    return [
        jnp.concatenate(
            [part(s, 0, 128), part(s + 2, 0, 128), part(s, 128, 192), part(s + 2, 128, 192)], -1
        )
        for s in range(2)
    ]


def whole_columns(sets):
    devices = [None] * 4
    for s in range(2):
        v = sets[s]
        devices[s] = jnp.concatenate([v[..., 0:128], v[..., 256:320]], -1)
        devices[s + 2] = jnp.concatenate([v[..., 128:256], v[..., 320:384]], -1)
    return jnp.concatenate(devices, -1)


def body(
    tokens,
    final_output_gradient,
    lengths,
    query_key_value_weight,
    output_projection_weight,
    biases,
    frozen_norm_gains,
    feedforward_in_weight,
    feedforward_bias,
    feedforward_out_weight,
    adapter_down_weights,
    adapter_up_weights,
):
    dp_size = lax.axis_size("dp")
    t = lax.axis_index("tensor")
    shard = lax.axis_index("dp")
    core = t & 1
    upper = t >> 1
    piece_rows = MODEL_WIDTH // dp_size
    pieces_fit = piece_rows % 16 == 0 and dp_size & (dp_size - 1) == 0

    meta = jnp.concatenate(
        [jnp.cumsum(lengths[0]), jnp.stack([t, shard]).astype(jnp.int32)]
    ).astype(jnp.int32)

    def of_core(value):
        first, second = set_columns(value)
        return jnp.where(core == 0, first, second)

    up = of_core(adapter_up_weights.astype(F32) * 2.0).astype(BF16)
    up_pad = [
        jnp.stack(
            [
                jnp.pad(up[l, 0], ((0, 120), (0, 0))),
                jnp.pad(up[l, 1], ((8, 112), (0, 0))),
            ]
        )
        for l in range(ENCODER_LAYERS)
    ]
    head_bias = of_core(biases[:, 0:2])
    adapter = [
        jnp.pad(
            jnp.concatenate([adapter_down_weights[l, 0], adapter_down_weights[l, 1]], -1),
            ((0, 0), (0, 112)),
        )
        for l in range(ENCODER_LAYERS)
    ]
    vecs = [
        jnp.concatenate([biases[l, 2:6], frozen_norm_gains[l], jnp.zeros((2, MODEL_WIDTH), F32)])
        for l in range(ENCODER_LAYERS)
    ]

    def attention_weights(l):
        own = jnp.concatenate([query_key_value_weight[l], output_projection_weight[l][None]])
        other = swap(own, "tensor", 2)
        first = jnp.where(upper == 0, own, other)
        second = jnp.where(upper == 0, other, own)
        piece = jnp.concatenate(
            [first[..., :128], second[..., :128], first[..., 128:], second[..., 128:]], -1
        )
        if pieces_fit:
            return gather_pieces(piece)
        return [lax.all_gather(piece, "dp", axis=1, tiled=True)]

    def direct(own):
        sib = swap(own, "tensor", 1)
        other = swap(own, "tensor", 2)
        return [[own], [sib], [other], [swap(other, "tensor", 1)]]

    def ringed(own):
        sib = swap(own, "tensor", 1)
        piece = swap(
            lax.dynamic_slice_in_dim(own, shard * piece_rows, piece_rows, 0), "tensor", 2
        )
        pieces = gather_pieces(piece)
        return [[own], [sib], pieces, [swap(p, "tensor", 1) for p in pieces]]

    def feedforward_weights(l, ring_in, ring_out):
        parts = []
        for value, ring in (
            (feedforward_in_weight[l], ring_in),
            (feedforward_out_weight[l], ring_out),
        ):
            parts.append(ringed(value) if ring and pieces_fit else direct(value))
        return [parts[m][j] for j in range(4) for m in range(2)]

    def gather_rows(rows):
        other = swap(rows, "tensor", 2)
        return [rows, swap(rows, "tensor", 1), other, swap(other, "tensor", 1)]

    att_w = [attention_weights(0)]
    bias_rows = jnp.pad(feedforward_bias, ((0, 14), (0, 0)))
    first_rows = gather_rows(jnp.concatenate([tokens, bias_rows]))
    n_rows = tokens.shape[0]
    x = [[r[:n_rows] for r in first_rows]]
    ff_bias = [
        jnp.stack([r[n_rows + l] for r in first_rows]).astype(F32) for l in range(ENCODER_LAYERS)
    ]
    ff_w = [feedforward_weights(0, False, True)]
    att_w.append(attention_weights(1))
    ff_w.append(feedforward_weights(1, True, True))

    saved = []
    rows = tokens
    for l in range(ENCODER_LAYERS):
        if l > 0:
            x.append(gather_rows(rows))
        q, k, v, lse, c, own, sib = attention_forward(
            meta, x[l], att_w[l], adapter[l], up_pad[l], head_bias[l]
        )
        sib = swap(sib, "tensor", 1)
        f1, f2, slope, rows = feedforward_forward(
            meta, rows, own, sib, vecs[l], ff_bias[l], ff_w[l]
        )
        saved.append((q, k, v, lse, c, f1, f2, slope))

    gs = [final_output_gradient]
    small = [None] * ENCODER_LAYERS
    for l in reversed(range(ENCODER_LAYERS)):
        q, k, v, lse, c, f1, f2, slope = saved[l]
        g_first, g_low = feedforward_backward(meta, gs, f1, f2, slope, vecs[l], ff_w[l])
        p0, p1, p2, p3, grads = attention_backward(
            meta,
            x[l],
            att_w[l],
            g_low,
            swap(g_low, "tensor", 1),
            g_first,
            (q, k, v, lse, c),
            adapter[l],
            up_pad[l],
        )
        p3 = swap(p3, "tensor", 1)
        p1 = swap(p1, "tensor", 1)
        p2 = swap((p2.astype(F32) + p3.astype(F32)).astype(BF16), "tensor", 2)
        gs = [p0, p1, p2]
        small[l] = sum_all(grads)

    input_grad = sum(g.astype(F32) for g in gs).astype(BF16)
    both = jnp.stack(small)
    shape = (ENCODER_LAYERS, 2, ADAPTER_RANK, MODEL_WIDTH)
    grad_a = both[:, :16].reshape(shape).swapaxes(2, 3)
    grad_b = both[:, 16:].reshape(shape)
    grad_b = whole_columns([grad_b[..., :SET_COLS], grad_b[..., SET_COLS:]])
    return rows, input_grad, grad_a, grad_b


def solution(mesh):
    return jax.shard_map(
        body,
        mesh=mesh,
        in_specs=(
            P(("dp", "tensor"), None),
            P(("dp", "tensor"), None),
            P("dp", None),
            P(None, None, "dp", "tensor"),
            P(None, "dp", "tensor"),
            P(),
            P(),
            P(None, None, "tensor"),
            P(None, "tensor"),
            P(None, "tensor", None),
            P(),
            P(),
        ),
        out_specs=(P(("dp", "tensor"), None), P(("dp", "tensor"), None), P(), P()),
        check_vma=False,
    )
```

time: 1190 us -> 373 us (0.31)
  waiting for transfers between devices: 649 us -> 134 us
  matrix products: 259 us -> 0 us
  blocking collectives: 133 us -> 0 us
  Pallas kernels: 0 us -> 116 us
  starting transfers between devices: 2.18 us -> 73.7 us
  other arithmetic: 65.4 us -> 12.3 us
  loops' own time: 16.6 us -> 0 us
  local copies, waits for them, and re-layouts: 42.1 us -> 27.4 us
  between operations: 15.8 us -> 2.41 us
    reduce_scatter x12 -> x0, waiting for transfers between devices: 407 us -> none  [the longest x4 137 us: layer_forward(): lax.psum_scatter(jnp.dot(piece_rows, out_full, preferred_element_type=jnp...]
    dot_general x82 -> x0, matrix products: 240 us -> none  [the longest x4 31.3 us: layer_forward(): jnp.dot(piece_rows, out_full, preferred_element_type=jnp.float32)]
    ppermute x0 -> x96, waiting for transfers between devices: none -> 134 us  [swap(): return lax.ppermute(value, axis, [(i, i ^ flip) for i in range(size)])]
    all_gather x4 -> x0, blocking collectives: 133 us -> none  [the longest x2 68.6 us: frozen_weights(): lax.all_gather(query_key_value_weight[current_layer_index], 'dp', axis=1,...]
    all_gather x10 -> x0, waiting for transfers between devices: 124 us -> none  [the longest x4 50.1 us: layer_forward(): lax.all_gather(normed_low, 'tensor', axis=0, tiled=True)]
    psum x1 -> x0, waiting for transfers between devices: 117 us -> none  [body(): grad_a, grad_b = lax.psum((grad_a, grad_b), ('dp', 'tensor'))]
    pallas_call x0 -> x8, Pallas kernels: none -> 116 us  [the longest x2 41.4 us: attention_backward(): pl.pallas_call(functools.partial(attention_backward_kernel, n, slots, gro...]
    ppermute x0 -> x96, starting transfers between devices: none -> 73.7 us  [swap(): return lax.ppermute(value, axis, [(i, i ^ flip) for i in range(size)])]
  transfers between devices with their start and end apart: 23 -> 96, of which waited for: 21 -> 37; matrix products, arithmetic and copies ran while one was open for 9% -> 8% of each run, Pallas kernels for 0% -> 18%
where the time goes in v1:
time: 373 us; the launch traced here: 365 us
  waiting for transfers between devices  134 us (36%)
  Pallas kernels  116 us (31%)
  starting transfers between devices  73.7 us (20%)
  local copies, waits for them, and re-layouts  27.4 us (7%)
  other arithmetic  12.3 us (3%)
    ppermute x96, waiting for transfers between devices, swap(): return lax.ppermute(value, axis, [(i, i ^ flip) for i in range(size)])  134 us
    ppermute x96, starting transfers between devices, swap(): return lax.ppermute(value, axis, [(i, i ^ flip) for i in range(size)])  73.7 us
    pallas_call x2, Pallas kernels, attention_backward(): pl.pallas_call(functools.partial(attention_backward_kernel, n, slots, gro...  41.4 us
    pallas_call x2, Pallas kernels, attention_forward(): pl.pallas_call(functools.partial(attention_forward_kernel, n, slots, grou...  33.9 us
    pallas_call x2, Pallas kernels, feedforward_forward(): pl.pallas_call(functools.partial(feedforward_forward_kernel, counts, slot...  21.2 us
    pallas_call x2, Pallas kernels, feedforward_backward(): pl.pallas_call(functools.partial(feedforward_backward_kernel, counts, slo...  19.7 us
  transfers between devices with their start and end apart: 96, of which 37 were waited for; matrix products, arithmetic and copies ran while one was open for 8% of the time, Pallas kernels for 18%

profile of v1, /device:TPU:0, one launch (start us, length us, event | category | flops | bytes accessed | tf_op | source)
XLA Modules:
  0.0 365.4 jit_solution(1619921348962419898)
XLA Ops:
  7.0 3.4 fusion.7
  19.7 4.1 %collective-permute-start.52 = (bf16[96,768]{1,0:T(8,128)(2,1)}, bf16[96,768]{1,0:T(8,128)(2,1)S(1)}, u32[]{:S(2)}, u32[]{:S(2)}) collective-permute-start(bf16[96,768]{1,0:T(8,128)(2,1)} %collective-permute-done.46.refs_9_), channel_id=1, source_target_pairs={{0,24},{4,28},{8,16},{12,20},{16,8},{20,12},{24,0},{28,4},{1,25},{... | collective-permute-start | bytes 442376 | tf_op jit(solution)/shard_map/ppermute | solution.py:580
  28.8 3.8 %collective-permute-start.21 = (bf16[96,768]{1,0:T(8,128)(2,1)S(1)}, bf16[96,768]{1,0:T(8,128)(2,1)S(1)}, u32[]{:S(2)}, u32[]{:S(2)}) collective-permute-start(bf16[96,768]{1,0:T(8,128)(2,1)S(1)} %collective-permute-done.15.refs_10_.refs_12_), channel_id=1, source_target_pairs={{0,24},{4,28},{8,16},{12,20},{16,8},{20,12},{24,0},{28,4},{1,25},{... | collective-permute-start | bytes 442376 | tf_op jit(solution)/shard_map/ppermute | solution.py:580
  32.6 8.1 %collective-permute-done.50.refs_13_ = bf16[96,768]{1,0:T(8,128)(2,1)S(1)} collective-permute-done((bf16[96,768]{1,0:T(8,128)(2,1)}, bf16[96,768]{1,0:T(8,128)(2,1)S(1)}, u32[]{:S(2)}, u32[]{:S(2)}) %collective-permute-start.50) | collective-permute-done | bytes 147488 | tf_op jit(solution)/shard_map/ppermute | solution.py:580
  61.3 3.6 collective-permute-done.58.refs_21_
  79.1 24.1 %collective-permute-done.39.refs_8_ = bf16[4,96,384]{2,1,0:T(8,128)(2,1)} collective-permute-done((bf16[4,96,384]{2,1,0:T(8,128)(2,1)S(1)}, bf16[4,96,384]{2,1,0:T(8,128)(2,1)}, u32[]{:S(2)}, u32[]{:S(2)}) %collective-permute-start.39) | collective-permute-done | bytes 294944 | tf_op jit(solution)/shard_map/ppermute | solution.py:580
  104.2 12.7 %collective-permute-done.7.refs_8_ = bf16[4,96,384]{2,1,0:T(8,128)(2,1)} collective-permute-done((bf16[4,96,384]{2,1,0:T(8,128)(2,1)S(1)}, bf16[4,96,384]{2,1,0:T(8,128)(2,1)}, u32[]{:S(2)}, u32[]{:S(2)}) %collective-permute-start.7) | collective-permute-done | bytes 294944 | tf_op jit(solution)/shard_map/ppermute | solution.py:580
  120.5 3.1 collective-permute-done.22.refs_17_.refs_19_
  133.0 4.0 %collective-permute-done.10.refs_11_ = bf16[4,96,384]{2,1,0:T(8,128)(2,1)} collective-permute-done((bf16[4,96,384]{2,1,0:T(8,128)(2,1)}, bf16[4,96,384]{2,1,0:T(8,128)(2,1)}, u32[]{:S(2)}, u32[]{:S(2)}) %collective-permute-start.10) | collective-permute-done | bytes 294944 | tf_op jit(solution)/shard_map/ppermute | solution.py:580
  143.3 5.8 %collective-permute-done.6.refs_7_ = bf16[4,96,384]{2,1,0:T(8,128)(2,1)S(1)} collective-permute-done((bf16[4,96,384]{2,1,0:T(8,128)(2,1)}, bf16[4,96,384]{2,1,0:T(8,128)(2,1)S(1)}, u32[]{:S(2)}, u32[]{:S(2)}) %collective-permute-start.6) | collective-permute-done | bytes 294944 | tf_op jit(solution)/shard_map/ppermute | solution.py:580
  149.8 17.1 %attention_forward.2 = (bf16[512,384]{1,0:T(8,128)(2,1)}, bf16[1024,384]{1,0:T(8,128)(2,1)}, bf16[1024,384]{1,0:T(8,128)(2,1)}, f32[8,512]{1,0:T(8,128)}, bf16[5...) custom-call(s32[34]{0:T(128)} %pad_add_fusion.meta, bf16[256,768]{1,0:T(8,128)(2,1)} %refs_0_.7, ...), custom_call_target="tpu_custom_call" | custom-call | flops 6000000000 | bytes 8000000 | tf_op jit(solution)/shard_map/attention_forward/pallas_call | solution.py:195
  174.1 10.8 %feedforward_forward.2 = (f32[256,768]{1,0:T(8,128)}, f32[256,768]{1,0:T(8,128)}, bf16[4,256,768]{2,1,0:T(8,128)(2,1)}, bf16[256,768]{1,0:T(8,128)(2,1)}) custom-call(s32[34]{0:T(128)} %pad_add_fusion.meta, bf16[256,768]{1,0:T(8,128)(2,1)} %refs_0_.7, f32[256,768]{1,0:T(8,128)} %get-tuple-element.40.refs_1_, bf16[256,768]{1,0:T(8,128)(2,1)} %copy-done.44, ...), custom_call_target="tpu_custom_call" | custom-call | flops 6000000000 | bytes 12000000 | tf_op jit(solution)/shard_map/feedforward_forward/pallas_call | solution.py:501
  189.4 4.3 %collective-permute-done.61.refs_24_ = bf16[96,768]{1,0:T(8,128)(2,1)S(1)} collective-permute-done((bf16[96,768]{1,0:T(8,128)(2,1)S(1)}, bf16[96,768]{1,0:T(8,128)(2,1)S(1)}, u32[]{:S(2)}, u32[]{:S(2)}) %collective-permute-start.61) | collective-permute-done | bytes 147488 | tf_op jit(solution)/shard_map/ppermute | solution.py:580
  198.5 13.4 %collective-permute-done.57.refs_20_ = bf16[96,768]{1,0:T(8,128)(2,1)S(1)} collective-permute-done((bf16[96,768]{1,0:T(8,128)(2,1)S(1)}, bf16[96,768]{1,0:T(8,128)(2,1)S(1)}, u32[]{:S(2)}, u32[]{:S(2)}) %collective-permute-start.57) | collective-permute-done | bytes 147488 | tf_op jit(solution)/shard_map/ppermute | solution.py:580
  215.0 4.7 %collective-permute-done.38.refs_7_ = bf16[4,96,384]{2,1,0:T(8,128)(2,1)} collective-permute-done((bf16[4,96,384]{2,1,0:T(8,128)(2,1)}, bf16[4,96,384]{2,1,0:T(8,128)(2,1)}, u32[]{:S(2)}, u32[]{:S(2)}) %collective-permute-start.38) | collective-permute-done | bytes 294944 | tf_op jit(solution)/shard_map/ppermute | solution.py:580
  220.4 16.8 %attention_forward.3 = (bf16[512,384]{1,0:T(8,128)(2,1)}, bf16[1024,384]{1,0:T(8,128)(2,1)}, bf16[1024,384]{1,0:T(8,128)(2,1)}, f32[8,512]{1,0:T(8,128)}, bf16[5...) custom-call(s32[34]{0:T(128)} %pad_add_fusion.meta, bf16[256,768]{1,0:T(8,128)(2,1)} %get-tuple-element.42.refs_0_, ...), custom_call_target="tpu_custom_call" | custom-call | flops 6000000000 | bytes 8000000 | tf_op jit(solution)/shard_map/attention_forward/pallas_call | solution.py:195
  243.1 10.5 %feedforward_forward.3 = (f32[256,768]{1,0:T(8,128)}, f32[256,768]{1,0:T(8,128)}, bf16[4,256,768]{2,1,0:T(8,128)(2,1)}, bf16[256,768]{1,0:T(8,128)(2,1)}) custom-call(s32[34]{0:T(128)} %pad_add_fusion.meta, bf16[256,768]{1,0:T(8,128)(2,1)} %get-tuple-element.42.refs_0_, f32[256,768]{1,0:T(8,128)} %get-tuple-element.43.refs_1_, bf16[256,768]{1,0:T(8,128)(2,1)} %copy-done.45, ...), custom_call_target="tpu_custom_call" | custom-call | flops 6000000000 | bytes 12000000 | tf_op jit(solution)/shard_map/feedforward_forward/pallas_call | solution.py:501
  253.5 9.7 %feedforward_backward.2 = (f32[256,768]{1,0:T(8,128)}, bf16[256,768]{1,0:T(8,128)(2,1)}) custom-call(s32[34]{0:T(128)} %pad_add_fusion.meta, bf16[256,768]{1,0:T(8,128)(2,1)} %refs_0_.6, f32[256,768]{1,0:T(8,128)} %get-tuple-element.46.refs_1_, f32[256,768]{1,0:T(8,128)} %get-tuple-element.47.refs_2_, bf16[4,256,768]{2,1,0:T(8,128)(2,1)} %get-tuple-element.48.refs_3_, ...), custom_call_target="tpu_custom_call" | custom-call | flops 6000000000 | bytes 12000000 | tf_op jit(solution)/shard_map/feedforward_backward/pallas_call | solution.py:559
  266.0 20.7 %attention_backward.2 = (f32[256,768]{1,0:T(8,128)}, bf16[256,768]{1,0:T(8,128)(2,1)}, bf16[256,768]{1,0:T(8,128)(2,1)}, bf16[256,768]{1,0:T(8,128)(2,1)}, f32[32,768]{1,0:T(8,128)}) custom-call(s32[34]{0:T(128)} %pad_add_fusion.meta, bf16[256,768]{1,0:T(8,128)(2,1)} %get-tuple-element.42.refs_0_, bf16[256,768]{1,0:T(8,128)(2,1)} %copy-done.42, ...), custom_call_target="tpu_custom_call" | custom-call | flops 10000000000 | bytes 8000000 | tf_op jit(solution)/shard_map/attention_backward/pallas_call | solution.py:385
  290.3 10.7 %collective-permute-done.81.refs_2_ = bf16[256,768]{1,0:T(8,128)(2,1)S(1)} collective-permute-done((bf16[256,768]{1,0:T(8,128)(2,1)S(1)}, bf16[256,768]{1,0:T(8,128)(2,1)S(1)}, u32[]{:S(2)}, u32[]{:S(2)}) %collective-permute-start.81) | collective-permute-done | bytes 393248 | tf_op jit(solution)/shard_map/ppermute | solution.py:580
  301.7 10.0 %feedforward_backward.3 = (f32[256,768]{1,0:T(8,128)}, bf16[256,768]{1,0:T(8,128)(2,1)}) custom-call(s32[34]{0:T(128)} %pad_add_fusion.meta, f32[256,768]{1,0:T(8,128)} %get-tuple-element.56.refs_0_, bf16[256,768]{1,0:T(8,128)(2,1)} %copy-done.46, bf16[256,768]{1,0:T(8,128)(2,1)} %copy-done.48, f32[256,768]{1,0:T(8,128)} %get-tuple-element.60.refs_3_, ...), custom_call_target="tpu_custom_call" | custom-call | flops 6000000000 | bytes 12000000 | tf_op jit(solution)/shard_map/feedforward_backward/pallas_call | solution.py:559
  315.0 20.7 %attention_backward.3 = (f32[256,768]{1,0:T(8,128)}, bf16[256,768]{1,0:T(8,128)(2,1)}, bf16[256,768]{1,0:T(8,128)(2,1)}, bf16[256,768]{1,0:T(8,128)(2,1)}, f32[32,768]{1,0:T(8,128)}) custom-call(s32[34]{0:T(128)} %pad_add_fusion.meta, bf16[256,768]{1,0:T(8,128)(2,1)} %refs_0_.7, bf16[256,768]{1,0:T(8,128)(2,1)} %slice.289.refs_1_, ...), custom_call_target="tpu_custom_call" | custom-call | flops 10000000000 | bytes 8000000 | tf_op jit(solution)/shard_map/attention_backward/pallas_call | solution.py:385
  348.6 3.6 collective-permute-done.95
  355.3 4.4 %collective-permute-done.90 = f32[32,768]{1,0:T(8,128)S(1)} collective-permute-done((f32[32,768]{1,0:T(8,128)S(1)}, f32[32,768]{1,0:T(8,128)S(1)}, u32[]{:S(2)}, u32[]{:S(2)}) %collective-permute-start.90) | collective-permute-done | bytes 98336 | tf_op jit(solution)/shard_map/ppermute | solution.py:580
  (473 shorter events, 133.1 us)
Async XLA Ops:
  25.2 18.6 %collective-permute-start.47 = (bf16[96,768]{1,0:T(8,128)(2,1)}, bf16[96,768]{1,0:T(8,128)(2,1)S(1)}, u32[]{:S(2)}, u32[]{:S(2)}) collective-permute-start(bf16[96,768]{1,0:T(8,128)(2,1)} %collective-permute-done.46.refs_9_), channel_id=1, source_target_pairs={{0,4},{4,0},{8,12},{12,8},{16,20},{20,16},{24,28},{28,24},{1,5},{5... | collective-permute-start | bytes 442376 | tf_op jit(solution)/shard_map/ppermute | solution.py:580
  27.6 18.8 %collective-permute-start.24 = (bf16[96,768]{1,0:T(8,128)(2,1)S(1)}, bf16[96,768]{1,0:T(8,128)(2,1)S(1)}, u32[]{:S(2)}, u32[]{:S(2)}) collective-permute-start(bf16[96,768]{1,0:T(8,128)(2,1)S(1)} %collective-permute-done.15.refs_10_.refs_12_), channel_id=1, source_target_pairs={{0,1},{1,0},{2,3},{3,2},{4,5},{5,4},{6,7},{7,6},{8,9},{9,8},{10,11... | collective-permute-start | bytes 442376 | tf_op jit(solution)/shard_map/ppermute | solution.py:580
  28.8 19.1 %collective-permute-start.21 = (bf16[96,768]{1,0:T(8,128)(2,1)S(1)}, bf16[96,768]{1,0:T(8,128)(2,1)S(1)}, u32[]{:S(2)}, u32[]{:S(2)}) collective-permute-start(bf16[96,768]{1,0:T(8,128)(2,1)S(1)} %collective-permute-done.15.refs_10_.refs_12_), channel_id=1, source_target_pairs={{0,24},{4,28},{8,16},{12,20},{16,8},{20,12},{24,0},{28,4},{1,25},{... | collective-permute-start | bytes 442376 | tf_op jit(solution)/shard_map/ppermute | solution.py:580
  46.3 23.1 %collective-permute-start.1 = (bf16[272,768]{1,0:T(8,128)(2,1)S(1)}, bf16[272,768]{1,0:T(8,128)(2,1)}, u32[]{:S(2)}, u32[]{:S(2)}) collective-permute-start(bf16[272,768]{1,0:T(8,128)(2,1)S(1)} %fusion.1), channel_id=1, source_target_pairs={{0,2},{1,3},{2,0},{3,1},{4,6},{5,7},{6,4},{7,5},{8,10},{9,11},{10,... | collective-permute-start | bytes 1253384 | tf_op jit(solution)/shard_map/ppermute | solution.py:580
  47.9 23.0 %collective-permute-start = (bf16[272,768]{1,0:T(8,128)(2,1)S(1)}, bf16[272,768]{1,0:T(8,128)(2,1)S(1)}, u32[]{:S(2)}, u32[]{:S(2)}) collective-permute-start(bf16[272,768]{1,0:T(8,128)(2,1)S(1)} %fusion.1), channel_id=1, source_target_pairs={{0,1},{1,0},{2,3},{3,2},{4,5},{5,4},{6,7},{7,6},{8,9},{9,8},{10,11... | collective-permute-start | bytes 1253384 | tf_op jit(solution)/shard_map/ppermute | solution.py:580
  67.0 36.2 %collective-permute-start.39 = (bf16[4,96,384]{2,1,0:T(8,128)(2,1)S(1)}, bf16[4,96,384]{2,1,0:T(8,128)(2,1)}, u32[]{:S(2)}, u32[]{:S(2)}) collective-permute-start(bf16[4,96,384]{2,1,0:T(8,128)(2,1)S(1)} %pad_maximum_fusion.1.refs_4_), channel_id=1, source_target_pairs={{0,16},{4,20},{8,24},{12,28},{16,0},{20,4},{24,8},{28,12},{1,17},{... | collective-permute-start | bytes 884744 | tf_op jit(solution)/shard_map/ppermute | solution.py:580
  67.1 36.1 %collective-permute-start.37 = (bf16[4,96,384]{2,1,0:T(8,128)(2,1)S(1)}, bf16[4,96,384]{2,1,0:T(8,128)(2,1)}, u32[]{:S(2)}, u32[]{:S(2)}) collective-permute-start(bf16[4,96,384]{2,1,0:T(8,128)(2,1)S(1)} %pad_maximum_fusion.1.refs_4_), channel_id=1, source_target_pairs={{0,8},{4,12},{8,0},{12,4},{16,24},{20,28},{24,16},{28,20},{1,9},{5... | collective-permute-start | bytes 884744 | tf_op jit(solution)/shard_map/ppermute | solution.py:580
  69.5 33.8 %collective-permute-start.36 = (bf16[4,96,384]{2,1,0:T(8,128)(2,1)S(1)}, bf16[4,96,384]{2,1,0:T(8,128)(2,1)}, u32[]{:S(2)}, u32[]{:S(2)}) collective-permute-start(bf16[4,96,384]{2,1,0:T(8,128)(2,1)S(1)} %pad_maximum_fusion.1.refs_4_), channel_id=1, source_target_pairs={{0,4},{4,0},{8,12},{12,8},{16,20},{20,16},{24,28},{28,24},{1,5},{5... | collective-permute-start | bytes 884744 | tf_op jit(solution)/shard_map/ppermute | solution.py:580
  71.0 32.3 %collective-permute-start.9 = (bf16[4,96,384]{2,1,0:T(8,128)(2,1)S(1)}, bf16[4,96,384]{2,1,0:T(8,128)(2,1)}, u32[]{:S(2)}, u32[]{:S(2)}) collective-permute-start(bf16[4,96,384]{2,1,0:T(8,128)(2,1)S(1)} %pad_maximum_fusion.refs_4_), channel_id=1, source_target_pairs={{0,24},{4,28},{8,16},{12,20},{16,8},{20,12},{24,0},{28,4},{1,25},{... | collective-permute-start | bytes 884744 | tf_op jit(solution)/shard_map/ppermute | solution.py:580
  76.8 60.7 %collective-permute-start.14 = (bf16[768,768]{1,0:T(8,128)(2,1)S(1)}, bf16[768,768]{1,0:T(8,128)(2,1)}, u32[]{:S(2)}, u32[]{:S(2)}) collective-permute-start(bf16[768,768]{1,0:T(8,128)(2,1)S(1)} %copy-done.7), channel_id=1, source_target_pairs={{0,2},{1,3},{2,0},{3,1},{4,6},{5,7},{6,4},{7,5},{8,10},{9,11},{10,... | collective-permute-start | bytes 3538952 | tf_op jit(solution)/shard_map/ppermute | solution.py:580
  130.9 18.2 %collective-permute-start.6 = (bf16[4,96,384]{2,1,0:T(8,128)(2,1)}, bf16[4,96,384]{2,1,0:T(8,128)(2,1)S(1)}, u32[]{:S(2)}, u32[]{:S(2)}) collective-permute-start(bf16[4,96,384]{2,1,0:T(8,128)(2,1)} %collective-permute-done.5.refs_6_), channel_id=1, source_target_pairs={{0,4},{4,0},{8,12},{12,8},{16,20},{20,16},{24,28},{28,24},{1,5},{5... | collective-permute-start | bytes 884744 | tf_op jit(solution)/shard_map/ppermute | solution.py:580
  137.0 34.5 %collective-permute-start.12 = (bf16[768,768]{1,0:T(8,128)(2,1)S(1)}, bf16[768,768]{1,0:T(8,128)(2,1)S(1)}, u32[]{:S(2)}, u32[]{:S(2)}) collective-permute-start(bf16[768,768]{1,0:T(8,128)(2,1)S(1)} %copy-done.7), channel_id=1, source_target_pairs={{0,1},{1,0},{2,3},{3,2},{4,5},{5,4},{6,7},{7,6},{8,9},{9,8},{10,11... | collective-permute-start | bytes 3538952 | tf_op jit(solution)/shard_map/ppermute | solution.py:580
  137.0 34.6 %collective-permute-start.13 = (bf16[768,768]{1,0:T(8,128)(2,1)S(1)}, bf16[768,768]{1,0:T(8,128)(2,1)S(1)}, u32[]{:S(2)}, u32[]{:S(2)}) collective-permute-start(bf16[768,768]{1,0:T(8,128)(2,1)S(1)} %get-tuple-element.77.refs_6_.refs_8_), channel_id=1, source_target_pairs={{0,1},{1,0},{2,3},{3,2},{4,5},{5,4},{6,7},{7,6},{8,9},{9,8},{10,11... | collective-permute-start | bytes 3538952 | tf_op jit(solution)/shard_map/ppermute | solution.py:580
  137.5 34.9 %collective-permute-start.23 = (bf16[768,768]{1,0:T(8,128)(2,1)}, bf16[768,768]{1,0:T(8,128)(2,1)S(1)}, u32[]{:S(2)}, u32[]{:S(2)}) collective-permute-start(bf16[768,768]{1,0:T(8,128)(2,1)} %collective-permute-done.14.refs_9_.refs_11_), channel_id=1, source_target_pairs={{0,1},{1,0},{2,3},{3,2},{4,5},{5,4},{6,7},{7,6},{8,9},{9,8},{10,11... | collective-permute-start | bytes 3538952 | tf_op jit(solution)/shard_map/ppermute | solution.py:580
  143.2 23.7 %collective-permute-start.25 = (bf16[96,768]{1,0:T(8,128)(2,1)S(1)}, bf16[96,768]{1,0:T(8,128)(2,1)S(1)}, u32[]{:S(2)}, u32[]{:S(2)}) collective-permute-start(bf16[96,768]{1,0:T(8,128)(2,1)S(1)} %copy-done.58), channel_id=1, source_target_pairs={{0,1},{1,0},{2,3},{3,2},{4,5},{5,4},{6,7},{7,6},{8,9},{9,8},{10,11... | collective-permute-start | bytes 442376 | tf_op jit(solution)/shard_map/ppermute | solution.py:580
  149.1 17.9 %collective-permute-start.31 = (bf16[96,768]{1,0:T(8,128)(2,1)S(1)}, bf16[96,768]{1,0:T(8,128)(2,1)}, u32[]{:S(2)}, u32[]{:S(2)}) collective-permute-start(bf16[96,768]{1,0:T(8,128)(2,1)S(1)} %copy-done.78), channel_id=1, source_target_pairs={{0,1},{1,0},{2,3},{3,2},{4,5},{5,4},{6,7},{7,6},{8,9},{9,8},{10,11... | collective-permute-start | bytes 442376 | tf_op jit(solution)/shard_map/ppermute | solution.py:580
  193.7 20.0 %collective-permute-start.42 = (bf16[4,96,384]{2,1,0:T(8,128)(2,1)}, bf16[4,96,384]{2,1,0:T(8,128)(2,1)}, u32[]{:S(2)}, u32[]{:S(2)}) collective-permute-start(bf16[4,96,384]{2,1,0:T(8,128)(2,1)} %collective-permute-done.41.refs_10_), channel_id=1, source_target_pairs={{0,4},{4,0},{8,12},{12,8},{16,20},{20,16},{24,28},{28,24},{1,5},{5... | collective-permute-start | bytes 884744 | tf_op jit(solution)/shard_map/ppermute | solution.py:580
  194.7 19.0 %collective-permute-start.40 = (bf16[4,96,384]{2,1,0:T(8,128)(2,1)}, bf16[4,96,384]{2,1,0:T(8,128)(2,1)}, u32[]{:S(2)}, u32[]{:S(2)}) collective-permute-start(bf16[4,96,384]{2,1,0:T(8,128)(2,1)} %collective-permute-done.39.refs_8_), channel_id=1, source_target_pairs={{0,4},{4,0},{8,12},{12,8},{16,20},{20,16},{24,28},{28,24},{1,5},{5... | collective-permute-start | bytes 884744 | tf_op jit(solution)/shard_map/ppermute | solution.py:580
  197.9 21.8 %collective-permute-start.32 = (bf16[256,768]{1,0:T(8,128)(2,1)}, bf16[256,768]{1,0:T(8,128)(2,1)S(1)}, u32[]{:S(2)}, u32[]{:S(2)}) collective-permute-start(bf16[256,768]{1,0:T(8,128)(2,1)} %get-tuple-element.42.refs_0_), channel_id=1, source_target_pairs={{0,1},{1,0},{2,3},{3,2},{4,5},{5,4},{6,7},{7,6},{8,9},{9,8},{10,11... | collective-permute-start | bytes 1179656 | tf_op jit(solution)/shard_map/ppermute | solution.py:580
  198.0 22.2 %collective-permute-start.34 = (bf16[256,768]{1,0:T(8,128)(2,1)S(1)}, bf16[256,768]{1,0:T(8,128)(2,1)}, u32[]{:S(2)}, u32[]{:S(2)}) collective-permute-start(bf16[256,768]{1,0:T(8,128)(2,1)S(1)} %collective-permute-done.33.refs_2_), channel_id=1, source_target_pairs={{0,1},{1,0},{2,3},{3,2},{4,5},{5,4},{6,7},{7,6},{8,9},{9,8},{10,11... | collective-permute-start | bytes 1179656 | tf_op jit(solution)/shard_map/ppermute | solution.py:580
  213.7 27.7 %collective-permute-start.44 = (bf16[768,768]{1,0:T(8,128)(2,1)S(1)}, bf16[768,768]{1,0:T(8,128)(2,1)S(1)}, u32[]{:S(2)}, u32[]{:S(2)}) collective-permute-start(bf16[768,768]{1,0:T(8,128)(2,1)S(1)} %copy-done.8), channel_id=1, source_target_pairs={{0,1},{1,0},{2,3},{3,2},{4,5},{5,4},{6,7},{7,6},{8,9},{9,8},{10,11... | collective-permute-start | bytes 3538952 | tf_op jit(solution)/shard_map/ppermute | solution.py:580
  213.8 27.7 %collective-permute-start.45 = (bf16[768,768]{1,0:T(8,128)(2,1)S(1)}, bf16[768,768]{1,0:T(8,128)(2,1)S(1)}, u32[]{:S(2)}, u32[]{:S(2)}) collective-permute-start(bf16[768,768]{1,0:T(8,128)(2,1)S(1)} %copy-done.6), channel_id=1, source_target_pairs={{0,1},{1,0},{2,3},{3,2},{4,5},{5,4},{6,7},{7,6},{8,9},{9,8},{10,11... | collective-permute-start | bytes 3538952 | tf_op jit(solution)/shard_map/ppermute | solution.py:580
  219.7 18.1 %collective-permute-start.69 = (bf16[96,768]{1,0:T(8,128)(2,1)}, bf16[96,768]{1,0:T(8,128)(2,1)S(1)}, u32[]{:S(2)}, u32[]{:S(2)}) collective-permute-start(bf16[96,768]{1,0:T(8,128)(2,1)} %collective-permute-done.53.refs_16_), channel_id=1, source_target_pairs={{0,1},{1,0},{2,3},{3,2},{4,5},{5,4},{6,7},{7,6},{8,9},{9,8},{10,11... | collective-permute-start | bytes 442376 | tf_op jit(solution)/shard_map/ppermute | solution.py:580
  313.6 22.2 %collective-permute-start.92 = (f32[32,768]{1,0:T(8,128)S(1)}, f32[32,768]{1,0:T(8,128)S(1)}, u32[]{:S(2)}, u32[]{:S(2)}) collective-permute-start(f32[32,768]{1,0:T(8,128)S(1)} %add.71), channel_id=1, source_target_pairs={{0,2},{1,3},{2,0},{3,1},{4,6},{5,7},{6,4},{7,5},{8,10},{9,11},{10,... | collective-permute-start | bytes 294920 | tf_op jit(solution)/shard_map/ppermute | solution.py:580
  (178 other events, 2828.5 us)
